TPU v7x, 512 devices: a whole 4x8x8 slice. The times are simulated.
512 devices in a mesh: pop: 32 (over x, y), mp: 16 (over z, core).
Axes of the slice: x: 4, y: 8, z: 8, core: 2. Of those that a mesh axis runs over, the one named last changes fastest.
Arguments:
- prompt_states: bfloat16 [512, 256, 3584], P(('pop', 'mp')), may hold values from -192 to 192
- norm_gain: float32 [3584], replicated, may hold values from 0.1 to 1.9
- kv_weight: bfloat16 [3584, 1024], P('mp'), may hold values from -0.09375 to 0.09375
- probe_keys: float32 [4, 128], replicated, may hold values from -6 to 6
- probe_values: float32 [4, 128], replicated, may hold values from -6 to 6
- down_factors: bfloat16 [512, 4, 3584], P(('pop', 'mp')), may hold values from -6 to 6
- up_factors: bfloat16 [512, 4, 1024], P(('pop', 'mp')), may hold values from -6 to 6
- group_ids: int32 [512], P(('pop', 'mp')), may hold values from 0 to 31, as said below
Outputs:
- fitness: float32 [512], P(('pop', 'mp'))
- update: float32 [3584, 1024], P('mp')
Inputs may be any that keep to these rules, and one draw needn't show every extreme that they name: `group_ids`: each group holds exactly 16 members.
All inputs are finite; a program needn't handle non-finite values.
Results may differ from a plain program's by a relative error of at most 0.0037.
Values may be sent and summed in bfloat16 or wider, within the bound.
No kernel may reach another device: no remote copies, remote signals or barrier semaphores. Data moves between devices by JAX's collectives and lax.ppermute only.
A program may use at most 64 MiB of HBM per device.

v0:
```python
import math

import jax
import jax.numpy as jnp
from jax import lax
from jax.sharding import PartitionSpec as P

KV_HEADS = 4
HEAD = 128
RANK = 4
GROUP_MEMBERS = 16


def weighted_product(fitness_rows, row_factors, column_factors):
    weighted = (fitness_rows[:, None, None] * row_factors.astype(jnp.float32)).reshape(
        -1, row_factors.shape[2]
    )
    upper = lax.optimization_barrier(weighted.astype(jnp.bfloat16))
    lower = (weighted - upper.astype(jnp.float32)).astype(jnp.bfloat16)
    columns = column_factors.reshape(-1, column_factors.shape[2])
    dims = (((0,), (0,)), ((), ()))
    first_part = lax.dot_general(upper, columns, dims, preferred_element_type=jnp.float32)
    second_part = lax.dot_general(lower, columns, dims, preferred_element_type=jnp.float32)
    return first_part + second_part


def local(
    prompt_states,
    norm_gain,
    kv_weight,
    probe_keys,
    probe_values,
    down_factors,
    up_factors,
    group_ids,
):
    states = prompt_states[0].astype(jnp.float32)
    tok_count = states.shape[0]
    scale = lax.rsqrt(jnp.mean(states * states, axis=-1, keepdims=True) + 1e-06)
    normed = (states * scale * norm_gain).astype(jnp.bfloat16)
    base = jnp.dot(
        normed,
        lax.all_gather(kv_weight, "mp", axis=0, tiled=True),
        preferred_element_type=jnp.float32,
    )
    low = jnp.dot(normed, down_factors[0].T, preferred_element_type=jnp.float32)
    projected = base + 0.0025 * jnp.dot(
        low, up_factors[0].astype(jnp.float32), precision=lax.Precision.HIGHEST
    )
    half = KV_HEADS * HEAD
    keys = projected[:, :half].reshape(tok_count, KV_HEADS, HEAD)
    values = projected[:, half:].reshape(tok_count, KV_HEADS, HEAD)
    key_score = jnp.einsum(
        "thd,hd->th", keys, probe_keys, precision=lax.Precision.HIGHEST
    ) / math.sqrt(HEAD)
    value_score = jnp.einsum(
        "thd,hd->th", values, probe_values, precision=lax.Precision.HIGHEST
    ) / math.sqrt(HEAD)
    reward = jnp.sum(jnp.tanh(key_score) * value_score) / tok_count
    members = lax.axis_size("pop") * lax.axis_size("mp")
    group_count = members // GROUP_MEMBERS
    onehot = (group_ids[0] == jnp.arange(group_count, dtype=jnp.int32)).astype(jnp.float32)
    sums = lax.psum(onehot * reward, ("pop", "mp"))
    baseline = sums / GROUP_MEMBERS
    centered = reward - jnp.sum(onehot * baseline)
    spread = lax.psum(centered * centered, ("pop", "mp")) / members
    fitness_value = centered / jnp.sqrt(spread + 1e-05)
    fitness_shard = jnp.reshape(fitness_value, (1,))
    row_parts = lax.all_to_all(down_factors, "mp", split_axis=2, concat_axis=0, tiled=True)
    all_rows = lax.all_gather(row_parts, "pop", axis=0, tiled=True)
    all_columns = lax.all_gather(up_factors, ("pop", "mp"), axis=0, tiled=True)
    all_fit = lax.all_gather(fitness_shard, ("pop", "mp"), axis=0, tiled=True)
    update = weighted_product(all_fit, all_rows, all_columns)
    return (fitness_shard, update / math.sqrt(RANK * members))


def solution(mesh):
    in_specs = (
        P(("pop", "mp"), None, None),
        P(),
        P("mp", None),
        P(),
        P(),
        P(("pop", "mp"), None, None),
        P(("pop", "mp"), None, None),
        P(("pop", "mp")),
    )
    out_specs = (P(("pop", "mp")), P("mp", None))
    return jax.shard_map(local, mesh=mesh, in_specs=in_specs, out_specs=out_specs, check_vma=False)
```

profile of v0, /device:TPU:26, one launch (start us, length us, event | category | flops | bytes accessed | tf_op | source)
XLA Modules:
  0.0 441.5 jit_solution(6713040176948268980)
XLA Ops:
  7.2 0.0 copy-start
  7.2 0.0 all-gather.4.cloned.1.call-start
  7.2 0.7 all-gather.4.cloned.1.call-update
  7.9 0.0 all-gather.6.cloned.1.call-start
  8.0 0.7 all-gather.6.cloned.1.call-update
  8.7 0.0 copy-start.3
  8.7 0.0 copy-start.5
  8.7 3.7 copy.16
  12.4 0.5 broadcast.41
  12.9 19.7 %reduce.1 = bf16[3584,4]{1,0:T(8,128)(2,1)S(1)} reduce(bf16[3584,1,4]{2,1,0:T(2,128)(2,1)S(1)} %bitcast.69, bf16[]{:T(256)} %broadcast.41), dimensions={1}, to_apply=%bitcast.56.reduce_sub_computation | reduce | bytes 57346
  32.6 1.5 reshape.58
  34.1 10.4 %all-to-all-start = ((bf16[16,2,448]{2,1,0:T(2,128)(2,1)}), bf16[16,2,448]{2,1,0:T(2,128)(2,1)S(1)}, u32[]{:S(2)}, u32[]{:S(2)}) async-start(bf16[16,2,448]{2,1,0:T(2,128)(2,1)} %reshape.58), calls=%async_computation | async-start | bytes 65536 | tf_op jit(solution)/shard_map/all_to_all | solution.py:69
  44.5 2.0 fusion.2
  46.6 0.0 copy-done.3
  46.6 0.0 copy-done.5
  46.6 2.2 fusion.8
  49.5 3.0 all-to-all-done
  52.5 2.1 reshape.59
  54.6 1.8 copy.17
  56.4 0.1 all_to_all.14
  56.6 0.0 copy-start.2
  56.6 13.1 %all-gather.4.cloned.1.call-done = bf16[3584,1024]{1,0:T(8,128)(2,1)} async-done(((bf16[224,1024]{1,0:T(8,128)(2,1)}), bf16[3584,1024]{1,0:T(8,128)(2,1)}) %all-gather.4.cloned.1.call-update) | async-done | bytes 7340048 | tf_op jit(solution)/shard_map/all_gather | solution.py:43
  69.6 5.7 %fusion.10 = f32[256,1024]{1,0:T(8,128)S(1)} fusion(bf16[3584,1024]{1,0:T(8,128)(2,1)} %all-gather.4.cloned.1.call-done, bf16[1,256,3584]{2,1,0:T(8,128)(2,1)} %param.8, f32[3584]{0:T(1024)S(1)} %copy-done.5, f32[256]{0:T(256)S(1)} %add_rsqrt_fusion), kind=kOutput, calls=%fused_computation.13 | convolution fusion | flops 1882718208 | bytes 10238976 | tf_op jit(solution)/shard_map/dot_general | solution.py:41
  75.4 0.0 copy-done.2
  75.4 0.0 copy-start.4
  75.4 0.7 fusion.16
  76.1 0.1 slice_bitcast_fusion.1
  76.2 0.0 copy-done
  76.2 0.5 fusion.18
  76.7 0.0 copy-done.4
  76.8 0.6 fusion.21
  77.3 0.6 fusion.27
  78.6 49.4 %all-gather = bf16[512,1,4,224]{3,2,1,0:T(4,128)(2,1)S(1)} all-gather(bf16[16,1,4,224]{3,2,1,0:T(4,128)(2,1)S(1)} %copy.18), channel_id=2, replica_groups=mesh['pop'=32,'mp'=16] {'pop'}, dimensions={0}, use_global_device_ids=true | all-gather | bytes 946176 | tf_op jit(solution)/shard_map/all_gather | solution.py:70
  128.0 96.1 %psum.14 = f32[32]{0:T(128)S(1)} all-reduce(f32[32]{0:T(128)S(1)} %compare_select_fusion.1), channel_id=1, replica_groups=mesh['pop'=32,'mp'=16] {'pop','mp'}, use_global_device_ids=true, to_apply=%region_2.0 | all-reduce | flops 32 | bytes 256 | tf_op jit(solution)/shard_map/psum | solution.py:63
  224.1 0.6 fusion.29
  225.4 0.0 all-gather.6.cloned.1.call-done
  225.4 6.9 %reshape.48 = bf16[2048,1024]{1,0:T(8,128)(2,1)} reshape(bf16[512,4,1024]{2,1,0:T(4,128)(2,1)} %all-gather.6.cloned.1.call-done) | data formatting | bytes 8388608 | tf_op jit(solution)/shard_map/reshape | solution.py:20
  232.3 94.4 %psum.15 = f32[]{:T(128)} all-reduce(f32[]{:T(128)S(6)} %mul.74), channel_id=1, replica_groups=mesh['pop'=32,'mp'=16] {'pop','mp'}, use_global_device_ids=true, to_apply=%region_4.0 | all-reduce | flops 1 | bytes 8 | tf_op jit(solution)/shard_map/psum | solution.py:66
  327.5 0.1 dynamic-update-slice
  327.6 95.8 %all-reduce = f32[512]{0:T(512)S(1)} all-reduce(f32[512]{0:T(512)S(1)} %dynamic-update-slice), channel_id=1, replica_groups=mesh['pop'=32,'mp'=16] {'pop','mp'}, use_global_device_ids=true, to_apply=%add | all-reduce | flops 512 | bytes 4096
  423.3 2.5 convert_multiply_fusion.1
  425.9 2.0 reshape.47
  427.8 0.1 convert_element_type.38
  428.0 0.0 copy-start.1
  428.0 3.5 fusion.30
  431.4 0.0 copy-done.1
  431.5 2.1 fusion.17
  (4 shorter events, 0.0 us)
Async XLA Ops:
  7.2 69.0 %copy-start = (f32[4,128]{1,0:T(4,128)S(1)}, f32[4,128]{1,0:T(4,128)}, u32[]{:S(2)}) copy-start(f32[4,128]{1,0:T(4,128)} %param.12) | copy-start | bytes 6148
  7.2 62.5 %all-gather.4.cloned.1.call-start = ((), (), s32[]{:S(2)}) async-start(), calls=%async_computation.1 | async-start | bytes 7798784 | tf_op jit(solution)/shard_map/all_gather | solution.py:43
  7.9 217.5 %all-gather.6.cloned.1.call-start = ((), (), s32[]{:S(2)}) async-start(), calls=%async_computation.2 | async-start | bytes 4202496 | tf_op jit(solution)/shard_map/all_gather | solution.py:71
  8.7 37.9 %copy-start.3 = (bf16[1,4,3584]{2,1,0:T(4,128)(2,1)S(1)}, bf16[1,4,3584]{2,1,0:T(4,128)(2,1)}, u32[]{:S(2)}) copy-start(bf16[1,4,3584]{2,1,0:T(4,128)(2,1)} %param.13) | copy-start | bytes 86020
  8.7 37.9 %copy-start.5 = (f32[3584]{0:T(1024)S(1)}, f32[3584]{0:T(1024)}, u32[]{:S(2)}) copy-start(f32[3584]{0:T(1024)} %param.9) | copy-start | bytes 43012
  34.1 18.3 %all-to-all-start = ((bf16[16,2,448]{2,1,0:T(2,128)(2,1)}), bf16[16,2,448]{2,1,0:T(2,128)(2,1)S(1)}, u32[]{:S(2)}, u32[]{:S(2)}) async-start(bf16[16,2,448]{2,1,0:T(2,128)(2,1)} %reshape.58), calls=%async_computation | async-start | bytes 65536 | tf_op jit(solution)/shard_map/all_to_all | solution.py:69
  56.6 18.8 %copy-start.2 = (bf16[1,4,1024]{2,1,0:T(4,128)(2,1)S(1)}, bf16[1,4,1024]{2,1,0:T(4,128)(2,1)}, u32[]{:S(2)}) copy-start(bf16[1,4,1024]{2,1,0:T(4,128)(2,1)} %param.14) | copy-start | bytes 24580
  75.4 1.3 copy-start.4
  428.0 3.5 copy-start.1
Sparse Core Ops, SparseCore 0:
  10.1 59.4 all-gather.3
  73.8 115.8 all-gather.5
where the time goes:
time: 442 us
  blocking collectives  336 us (76%)
  other arithmetic  25.6 us (6%)
  local copies, waits for them, and re-layouts  18.9 us (4%)
  between operations  18 us (4%)
  waiting for transfers between devices  17.5 us (4%)
  matrix products  15.3 us (3%)
  starting transfers between devices  10.5 us (2%)
    psum x1, blocking collectives, local(): sums = lax.psum(onehot * reward, ('pop', 'mp'))  96.1 us
    unnamed x1, blocking collectives  95.8 us
    psum x1, blocking collectives, local(): spread = lax.psum(centered * centered, ('pop', 'mp')) / members  94.4 us
    all_gather x1, blocking collectives, local(): all_rows = lax.all_gather(row_parts, 'pop', axis=0, tiled=True)  49.4 us
    unnamed x1, other arithmetic  19.7 us
    all_gather x1, waiting for transfers between devices, local(): lax.all_gather(kv_weight, 'mp', axis=0, tiled=True)  13.1 us
    all_to_all x1, starting transfers between devices, local(): lax.all_to_all(down_factors, 'mp', split_axis=2, concat_axis=0, tiled=True)  10.4 us
  transfers between devices with their start and end apart: 3, of which 2 were waited for; matrix products, arithmetic and copies ran while one was open for 10% of the time, Pallas kernels for 0%

commit v1 on v0

v1 whole, which is shorter than its diff:
```python
import math

import jax
import jax.numpy as jnp
from jax import lax
from jax.experimental import pallas as pl
from jax.experimental.pallas import tpu as pltpu
from jax.sharding import Mesh
from jax.sharding import PartitionSpec as P

KV_HEADS = 4
HEAD = 128
RANK = 4
GROUP_MEMBERS = 16
LANES = 128
SUBLANES = 8
XY = ("x", "y")
ZC = ("z", "core")
ALL = ("x", "y", "z", "core")
VMEM = pl.BlockSpec(memory_space=pltpu.VMEM)
SMEM = pl.BlockSpec(memory_space=pltpu.SMEM)
F32 = jnp.float32
BF16 = jnp.bfloat16
CONTRACT_LANES = (((1,), (1,)), ((), ()))
CONTRACT_ROWS = (((0,), (0,)), ((), ()))


def three_parts(value):
    high = value.astype(BF16)
    rest = value - high.astype(F32)
    middle = rest.astype(BF16)
    low = rest - middle.astype(F32)
    return jnp.concatenate([high.astype(F32), middle.astype(F32), low], axis=0).astype(BF16)


def sum_parts(product):
    rows = product.shape[0] // 3
    return product[:rows] + (product[rows : 2 * rows] + product[2 * rows :])


def iota(shape, axis):
    return lax.broadcasted_iota(jnp.int32, shape, axis)


def one_hot(condition):
    return jnp.where(condition, 1.0, 0.0).astype(BF16)


def probe_kernel(weight, probe_keys, probe_values, up, down, weight_probe, up_probe, factors):
    copies, _, rows = weight_probe.shape
    probes = jnp.concatenate([probe_keys[...], probe_values[...]], axis=0)
    heads = probes.shape[0]
    wide = jnp.concatenate([probes] * heads, axis=1)
    own = iota(wide.shape, 1) // HEAD == iota(wide.shape, 0)
    probes = three_parts(jnp.where(own, wide, 0.0))
    product = sum_parts(lax.dot_general(probes, weight[...], CONTRACT_LANES, preferred_element_type=F32))
    weight_probe[...] = jnp.broadcast_to(product[None], weight_probe.shape)
    up_probe[...] = sum_parts(lax.dot_general(probes, up[...], CONTRACT_LANES, preferred_element_type=F32))

    half = up.shape[1] // 2
    select = iota((2 * RANK, RANK), 0), iota((2 * RANK, RANK), 1)
    upper = one_hot(select[0] == select[1])
    lower = one_hot(select[0] == select[1] + RANK)

    def place(which, block):
        return jnp.dot(which, block, preferred_element_type=F32)

    ups = (place(upper, up[:, :half]) + place(lower, up[:, half:])).astype(BF16)
    first = place(upper, down[...])
    second = place(lower, down[...])
    spare = jnp.zeros((2 * RANK, LANES), F32)
    second = jnp.concatenate([second, spare], axis=1)
    for i in range(copies):
        start = i * rows
        downs = first[:, start : start + LANES] + second[:, start + LANES : start + 2 * LANES]
        factors[i, :, :half] = ups
        factors[i, :, half:] = downs.astype(BF16)


def norm_kernel(states, gain, down, normed, low):
    values = states[...].astype(F32)
    scale = lax.rsqrt(jnp.mean(values * values, axis=-1, keepdims=True) + 1e-06)
    normed[...] = (values * scale * gain[...]).astype(BF16)
    low[...] = lax.dot_general(down[...], normed[...], CONTRACT_LANES, preferred_element_type=F32)


def reward_kernel(place, normed, low, weight_probe, up_probe, out):
    members = out.shape[0]
    probe = jnp.concatenate([weight_probe[i] for i in range(members)], axis=1)
    score = sum_parts(lax.dot_general(three_parts(probe), normed[...], CONTRACT_LANES, preferred_element_type=F32))
    extra = up_probe[:, 0:1] * low[0:1, :]
    for i in range(1, RANK):
        extra = extra + up_probe[:, i : i + 1] * low[i : i + 1, :]
    score = (score + 0.0025 * extra) * (1.0 / math.sqrt(HEAD))
    terms = jnp.tanh(score[:KV_HEADS]) * score[KV_HEADS:]
    reward = jnp.sum(jnp.sum(terms, axis=1, keepdims=True), axis=0, keepdims=True) * (1.0 / terms.shape[1])
    lane = iota(out.shape[1:], 1)
    group = place[2].astype(F32)
    row = jnp.where(lane == place[1], reward, 0.0) + jnp.where(lane == place[1] + members, group, 0.0)
    out[...] = jnp.broadcast_to(row[None], out.shape)


def relay_kernel(place, rows, out):
    row = jnp.sum(rows[...], axis=0)
    mine = iota(row.shape, 0) == place[0] % SUBLANES
    out[...] = jnp.broadcast_to(jnp.where(mine, row, 0.0)[None], out.shape)


def pack_kernel(factors, pieces):
    members, packed, width = factors.shape
    rows = members * packed
    count = members * RANK
    flat = factors[...].astype(F32).reshape(rows, width).astype(BF16)
    target = iota((rows, rows), 0)
    source = iota((rows, rows), 1)
    wanted = target % count // RANK * packed + target // count * RANK + target % RANK
    flat = jnp.dot(one_hot(source == wanted), flat, preferred_element_type=F32)
    half = width - LANES
    down = jnp.concatenate([flat[:count, half:], flat[count:, half:]], axis=1)
    targets = pieces.shape[0]
    column_parts = 2 * half // LANES
    row_parts = targets // column_parts
    share = (pieces.shape[2] - 16) // 2
    spare = jnp.zeros((count // 2, SUBLANES), F32)
    for i in range(row_parts):
        mine = down[:, i * share : (i + 1) * share]
        mine = jnp.concatenate([mine[: count // 2], spare, mine[count // 2 :], spare], axis=1).astype(BF16)
        for j in range(column_parts):
            first_row = j // (column_parts // 2) * count
            column = j % (column_parts // 2) * LANES
            columns = flat[first_row : first_row + count, column : column + LANES]
            pieces[i * column_parts + j, :count, :] = columns.astype(BF16)
            pieces[i * column_parts + j, count:, :] = mine


def update_kernel(place, rows, pieces, fitness, out):
    sources = rows.shape[0]
    table = jnp.sum(rows[...].reshape(sources // SUBLANES, SUBLANES, SUBLANES, LANES), axis=1)
    table = table.reshape(sources, LANES)
    count = pieces.shape[1] * 2 // 3
    members = count // RANK
    lane = iota(table.shape, 1)
    reward = jnp.where(lane < members, table, 0.0)
    group = jnp.where(lane < members, pltpu.roll(table, LANES - members, axis=1), -1.0)
    total = sources * members
    sums = [
        jnp.sum(jnp.where(group == float(i), reward, 0.0), axis=0, keepdims=True)
        for i in range(total // GROUP_MEMBERS)
    ]
    sums = jnp.sum(jnp.concatenate(sums, axis=0), axis=1, keepdims=True) * (1.0 / GROUP_MEMBERS)
    baseline = jnp.zeros_like(reward)
    for i in range(total // GROUP_MEMBERS):
        baseline = jnp.where(group == float(i), sums[i : i + 1, :], baseline)
    centered = jnp.where(lane < members, reward - baseline, 0.0)
    spread = jnp.sum(jnp.sum(centered * centered, axis=1, keepdims=True), axis=0, keepdims=True) * (1.0 / total)
    shaped = centered / jnp.sqrt(spread + 1e-05)
    own = jnp.where((iota(table.shape, 0) == place[0]) & (lane == place[1]), shaped, 0.0)
    fitness[...] = jnp.sum(jnp.sum(own, axis=1, keepdims=True), axis=0, keepdims=True)

    chosen = iota((count, LANES), 1) == iota((count, LANES), 0) // RANK
    weights = jnp.where(chosen[None], jnp.broadcast_to(shaped[:, None, :], (sources, count, LANES)), 0.0)
    weights = jnp.sum(weights, axis=2, keepdims=True)
    weighted = pieces[:, :count, :].astype(F32) * weights
    high = weighted.astype(BF16)
    low = (weighted - high.astype(F32)).astype(BF16)
    part = count // 2
    flat = sources * part
    columns = [
        block[:, start : start + part, :].reshape(flat, LANES) for start in (0, part) for block in (high, low)
    ]
    downs = pieces[:, count:, :].reshape(flat, LANES)
    product = lax.dot_general(downs, jnp.concatenate(columns, axis=1), CONTRACT_ROWS, preferred_element_type=F32)
    middle = LANES // 2
    first = product[:middle, :LANES] + product[:middle, LANES : 2 * LANES]
    second = product[middle:, 2 * LANES : 3 * LANES] + product[middle:, 3 * LANES :]
    block = ((first + second) * (1.0 / math.sqrt(RANK * total))).astype(BF16)
    out[...] = jnp.broadcast_to(block[None], out.shape)


def assemble_kernel(blocks, out):
    sources = blocks.shape[0]
    column_parts = out.shape[1] // LANES
    share = out.shape[0] * column_parts // sources
    for i in range(sources):
        row, column = i // column_parts * share, i % column_parts * LANES
        out[row : row + share, column : column + LANES] = blocks[i].astype(F32)[:share]


def call(kernel, out_shape, in_specs, *operands):
    many = isinstance(out_shape, (list, tuple))
    return pl.pallas_call(
        kernel,
        out_shape=out_shape,
        in_specs=in_specs,
        out_specs=[VMEM] * len(out_shape) if many else VMEM,
        compiler_params=pltpu.CompilerParams(vmem_limit_bytes=40 * 1024 * 1024),
    )(*operands)


def exchange(array, axes):
    return lax.all_to_all(array, axes, split_axis=0, concat_axis=0, tiled=True)


def local(
    prompt_states,
    norm_gain,
    kv_weight,
    probe_keys,
    probe_values,
    down_factors,
    up_factors,
    group_ids,
):
    pop = lax.axis_size(XY)
    mp = lax.axis_size(ZC)
    place = jnp.stack([lax.axis_index(XY), lax.axis_index(ZC), group_ids[0]]).astype(jnp.int32)
    states, down, up = prompt_states[0], down_factors[0], up_factors[0]
    tokens, width = states.shape
    columns = up.shape[1]
    rows = width // mp
    heads = 2 * KV_HEADS
    weight_probe, up_probe, factors = call(
        probe_kernel,
        [
            jax.ShapeDtypeStruct((mp, heads, rows), F32),
            jax.ShapeDtypeStruct((heads, RANK), F32),
            jax.ShapeDtypeStruct((mp, 2 * RANK, columns // 2 + LANES), BF16),
        ],
        [VMEM] * 5,
        kv_weight,
        probe_keys,
        probe_values,
        up,
        down,
    )
    weight_probe = exchange(weight_probe, ZC)
    factors = exchange(factors, ZC)
    normed, low = call(
        norm_kernel,
        [jax.ShapeDtypeStruct((tokens, width), BF16), jax.ShapeDtypeStruct((RANK, tokens), F32)],
        [VMEM] * 3,
        states,
        norm_gain[None],
        down,
    )
    reward = call(
        reward_kernel,
        jax.ShapeDtypeStruct((mp, SUBLANES, LANES), F32),
        [SMEM] + [VMEM] * 4,
        place,
        normed,
        low,
        weight_probe,
        up_probe,
    )
    reward = exchange(reward, ZC)
    count = mp * RANK
    pieces = call(pack_kernel, jax.ShapeDtypeStruct((pop, count * 3 // 2, LANES), BF16), [VMEM], factors)
    pieces = exchange(pieces, XY)
    reward = call(
        relay_kernel, jax.ShapeDtypeStruct((pop, SUBLANES, LANES), F32), [SMEM, VMEM], place, reward
    )
    reward = exchange(reward, XY)
    fitness, blocks = call(
        update_kernel,
        [jax.ShapeDtypeStruct((1, 1), F32), jax.ShapeDtypeStruct((pop, LANES // 2, LANES), BF16)],
        [SMEM, VMEM, VMEM],
        place,
        reward,
        pieces,
    )
    blocks = exchange(blocks, XY)
    update = call(assemble_kernel, jax.ShapeDtypeStruct((rows, columns), F32), [VMEM], blocks)
    return (fitness.reshape(1), update)


def solution(mesh):
    grid = Mesh(mesh.devices.reshape(4, 8, 8, 2), ALL)
    in_specs = (
        P(ALL, None, None),
        P(),
        P(ZC, None),
        P(),
        P(),
        P(ALL, None, None),
        P(ALL, None, None),
        P(ALL),
    )
    out_specs = (P(ALL), P(ZC, None))
    return jax.shard_map(local, mesh=grid, in_specs=in_specs, out_specs=out_specs, check_vma=False)
```

time: 442 us -> 124 us (0.28)
  the two profiles are of different devices: /device:TPU:26 before, /device:TPU:8 now
where the time goes in v1:
time: 124 us; the launch traced here: 123 us
  blocking collectives  60.3 us (49%)
  starting transfers between devices  24.1 us (19%)
  waiting for transfers between devices  22.5 us (18%)
  Pallas kernels  7.66 us (6%)
  local copies, waits for them, and re-layouts  6.79 us (5%)
  between operations  1.37 us (1%)
    all_to_all x3, blocking collectives, exchange(): return lax.all_to_all(array, axes, split_axis=0, concat_axis=0, tiled=True)  60.3 us
    all_to_all x3, starting transfers between devices, exchange(): return lax.all_to_all(array, axes, split_axis=0, concat_axis=0, tiled=True)  24.1 us
    all_to_all x3, waiting for transfers between devices, exchange(): return lax.all_to_all(array, axes, split_axis=0, concat_axis=0, tiled=True)  22.5 us
    pallas_call x7, Pallas kernels, call(): pl.pallas_call(kernel, out_shape=out_shape, in_specs=in_specs, out_specs=...  7.66 us
    unnamed x14, local copies, waits for them, and re-layouts  6.06 us
  transfers between devices with their start and end apart: 3, of which 3 were waited for; matrix products, arithmetic and copies ran while one was open for 1% of the time, Pallas kernels for 2%

profile of v1, /device:TPU:8, one launch (start us, length us, event | category | flops | bytes accessed | tf_op | source)
XLA Modules:
  0.0 122.8 jit_solution(10964560250688109775)
XLA Ops:
  0.6 0.0 copy-start.1
  0.6 1.0 copy-done.1
  1.7 0.0 copy-start.2
  1.7 0.7 copy-done.2
  2.4 0.0 copy-start.4
  2.4 0.7 copy-done.4
  3.1 0.0 copy-start.5
  3.1 0.7 copy-done.5
  3.8 0.0 copy-start.6
  3.8 0.7 copy-done.6
  4.5 1.1 shard_map.96
  5.5 10.4 %all-to-all-start = ((f32[16,8,224]{2,1,0:T(8,128)}), f32[16,8,224]{2,1,0:T(8,128)S(1)}, u32[]{:S(2)}, u32[]{:S(2)}) async-start(f32[16,8,224]{2,1,0:T(8,128)} %get-tuple-element.11), calls=%async_computation | async-start | bytes 262144 | tf_op jit(solution)/shard_map/all_to_all | solution.py:201
  16.6 0.7 broadcast_in_dim.3.gain
  17.4 0.0 copy-start
  17.4 1.5 %copy-done = bf16[1,256,3584]{2,1,0:T(8,128)(2,1)S(1)} copy-done((bf16[1,256,3584]{2,1,0:T(8,128)(2,1)S(1)}, bf16[1,256,3584]{2,1,0:T(8,128)(2,1)}, u32[]{:S(2)}) %copy-start) | copy-done | bytes 1835032
  18.9 0.0 copy-start.3
  18.9 0.7 copy-done.3
  19.6 1.0 shard_map.95
  20.6 0.1 pad_add_fusion.place
  20.7 4.0 %all-to-all-done.weight_probe = f32[16,8,224]{2,1,0:T(8,128)S(1)} async-done(((f32[16,8,224]{2,1,0:T(8,128)}), f32[16,8,224]{2,1,0:T(8,128)S(1)}, u32[]{:S(2)}, u32[]{:S(2)}) %all-to-all-start) | async-done | bytes 114720 | tf_op jit(solution)/shard_map/all_to_all | solution.py:201
  24.7 1.3 %shard_map.97 = f32[16,8,128]{2,1,0:T(8,128)S(1)} custom-call(s32[3]{0:T(128)S(1)} %pad_add_fusion.place, bf16[256,3584]{1,0:T(8,128)(2,1)S(1)} %get-tuple-element.9.normed, f32[4,256]{1,0:T(4,128)S(1)} %get-tuple-element.10.low, f32[16,8,224]{2,1,0:T(8,128)S(1)} %all-to-all-done.weight_probe, f32[8,4]{1,0:T(8,128)S(1)} %get-tuple-element.12.up_probe), custom_call_target="tpu_custom_call" | custom-call | tf_op jit(solution)/shard_map/pallas_call | solution.py:191
  26.0 10.9 %all_to_all.30.rows = f32[16,8,128]{2,1,0:T(8,128)S(1)} all-to-all(f32[16,8,128]{2,1,0:T(8,128)S(1)} %shard_map.97), channel_id=1, replica_groups=mesh['x'=4,'y'=8,'z'=8,'core'=2] {'z','core'}, dimensions={0} | all-to-all | bytes 131072 | tf_op jit(solution)/shard_map/all_to_all | solution.py:201
  36.9 3.5 %all-to-all-start.3 = ((bf16[16,8,640]{2,1,0:T(8,128)(2,1)}), bf16[16,8,640]{2,1,0:T(8,128)(2,1)S(1)}, u32[]{:S(2)}, u32[]{:S(2)}) async-start(bf16[16,8,640]{2,1,0:T(8,128)(2,1)} %get-tuple-element.13), calls=%async_computation.3 | async-start | bytes 327680 | tf_op jit(solution)/shard_map/all_to_all | solution.py:201
  40.5 1.2 shard_map.98
  41.7 8.0 %all-to-all-done.3.factors = bf16[16,8,640]{2,1,0:T(8,128)(2,1)S(1)} async-done(((bf16[16,8,640]{2,1,0:T(8,128)(2,1)}), bf16[16,8,640]{2,1,0:T(8,128)(2,1)S(1)}, u32[]{:S(2)}, u32[]{:S(2)}) %all-to-all-start.3) | async-done | bytes 163872 | tf_op jit(solution)/shard_map/all_to_all | solution.py:201
  49.6 10.2 %all-to-all-start.2 = ((f32[32,8,128]{2,1,0:T(8,128)}), f32[32,8,128]{2,1,0:T(8,128)S(1)}, u32[]{:S(2)}, u32[]{:S(2)}) async-start(f32[32,8,128]{2,1,0:T(8,128)} %shard_map.98), calls=%async_computation.2 | async-start | bytes 262144 | tf_op jit(solution)/shard_map/all_to_all | solution.py:201
  59.8 0.3 shard_map.99
  60.1 10.6 %all-to-all-done.2.rows = f32[32,8,128]{2,1,0:T(8,128)S(1)} async-done(((f32[32,8,128]{2,1,0:T(8,128)}), f32[32,8,128]{2,1,0:T(8,128)S(1)}, u32[]{:S(2)}, u32[]{:S(2)}) %all-to-all-start.2) | async-done | bytes 131104 | tf_op jit(solution)/shard_map/all_to_all | solution.py:201
  70.7 27.4 %all_to_all.31.pieces = bf16[32,96,128]{2,1,0:T(8,128)(2,1)S(1)} all-to-all(bf16[32,96,128]{2,1,0:T(8,128)(2,1)S(1)} %shard_map.99), channel_id=1, replica_groups=mesh['x'=4,'y'=8,'z'=8,'core'=2] {'x','y'}, dimensions={0} | all-to-all | bytes 1572864 | tf_op jit(solution)/shard_map/all_to_all | solution.py:201
  98.0 1.8 %shard_map.100 = (f32[1,1]{1,0:T(1,128)}, bf16[32,64,128]{2,1,0:T(8,128)(2,1)S(1)}) custom-call(s32[3]{0:T(128)S(1)} %pad_add_fusion.place, f32[32,8,128]{2,1,0:T(8,128)S(1)} %all-to-all-done.2.rows, bf16[32,96,128]{2,1,0:T(8,128)(2,1)S(1)} %all_to_all.31.pieces), custom_call_target="tpu_custom_call" | custom-call | tf_op jit(solution)/shard_map/pallas_call | solution.py:191
  99.8 22.0 %all_to_all.32.blocks = bf16[32,64,128]{2,1,0:T(8,128)(2,1)S(1)} all-to-all(bf16[32,64,128]{2,1,0:T(8,128)(2,1)S(1)} %get-tuple-element.15), channel_id=1, replica_groups=mesh['x'=4,'y'=8,'z'=8,'core'=2] {'x','y'}, dimensions={0} | all-to-all | bytes 1048576 | tf_op jit(solution)/shard_map/all_to_all | solution.py:201
  121.9 1.0 shard_map.101
Async XLA Ops:
  0.6 1.0 copy-start.1
  1.7 0.7 copy-start.2
  2.4 0.7 copy-start.4
  3.1 0.7 copy-start.5
  3.8 0.7 copy-start.6
  5.5 19.2 %all-to-all-start = ((f32[16,8,224]{2,1,0:T(8,128)}), f32[16,8,224]{2,1,0:T(8,128)S(1)}, u32[]{:S(2)}, u32[]{:S(2)}) async-start(f32[16,8,224]{2,1,0:T(8,128)} %get-tuple-element.11), calls=%async_computation | async-start | bytes 262144 | tf_op jit(solution)/shard_map/all_to_all | solution.py:201
  17.4 1.5 %copy-start = (bf16[1,256,3584]{2,1,0:T(8,128)(2,1)S(1)}, bf16[1,256,3584]{2,1,0:T(8,128)(2,1)}, u32[]{:S(2)}) copy-start(bf16[1,256,3584]{2,1,0:T(8,128)(2,1)} %param.8) | copy-start | bytes 5505028
  18.9 0.7 copy-start.3
  36.9 12.7 %all-to-all-start.3 = ((bf16[16,8,640]{2,1,0:T(8,128)(2,1)}), bf16[16,8,640]{2,1,0:T(8,128)(2,1)S(1)}, u32[]{:S(2)}, u32[]{:S(2)}) async-start(bf16[16,8,640]{2,1,0:T(8,128)(2,1)} %get-tuple-element.13), calls=%async_computation.3 | async-start | bytes 327680 | tf_op jit(solution)/shard_map/all_to_all | solution.py:201
  49.6 21.0 %all-to-all-start.2 = ((f32[32,8,128]{2,1,0:T(8,128)}), f32[32,8,128]{2,1,0:T(8,128)S(1)}, u32[]{:S(2)}, u32[]{:S(2)}) async-start(f32[32,8,128]{2,1,0:T(8,128)} %shard_map.98), calls=%async_computation.2 | async-start | bytes 262144 | tf_op jit(solution)/shard_map/all_to_all | solution.py:201

commit v2 on v1

v2 whole, which is shorter than its diff:
```python
import math

import jax
import jax.numpy as jnp
from jax import lax
from jax.experimental import pallas as pl
from jax.experimental.pallas import tpu as pltpu
from jax.sharding import Mesh
from jax.sharding import PartitionSpec as P

KV_HEADS = 4
HEAD = 128
RANK = 4
GROUP_MEMBERS = 16
LANES = 128
SUBLANES = 8
XY = ("x", "y")
ZC = ("z", "core")
ALL = ("x", "y", "z", "core")
VMEM = pl.BlockSpec(memory_space=pltpu.VMEM)
SMEM = pl.BlockSpec(memory_space=pltpu.SMEM)
F32 = jnp.float32
BF16 = jnp.bfloat16
CONTRACT_LANES = (((1,), (1,)), ((), ()))
CONTRACT_ROWS = (((0,), (0,)), ((), ()))


def bf16_parts(value, count):
    parts = []
    for _ in range(count):
        part = value.astype(BF16).astype(F32)
        parts.append(part)
        value = value - part
    return parts


def iota(shape, axis):
    return lax.broadcasted_iota(jnp.int32, shape, axis)


def sum_all(value):
    return jnp.sum(jnp.sum(value, axis=1, keepdims=True), axis=0, keepdims=True)


def pair_upper(even, odd):
    return jnp.where(iota(even.shape, even.ndim - 2) < RANK, even, pltpu.roll(odd, RANK, axis=odd.ndim - 2))


def pair_lower(even, odd):
    return jnp.where(iota(even.shape, even.ndim - 2) < RANK, pltpu.roll(even, RANK, axis=even.ndim - 2), odd)


def probe_kernel(weight_hbm, keys_hbm, values_hbm, up_hbm, down_hbm, up_probe, out, *scratch):
    buffers, sems = scratch[:5], scratch[5]
    sources = (weight_hbm, keys_hbm, values_hbm, up_hbm, down_hbm)
    copies = [pltpu.make_async_copy(a, b, sems.at[i]) for i, (a, b) in enumerate(zip(sources, buffers))]
    for copy in copies:
        copy.start()
    for copy in copies:
        copy.wait()
    weight, probe_keys, probe_values, up, down = buffers
    devices, _, rows = out.shape
    probes = jnp.concatenate([probe_keys[...], probe_values[...]], axis=0)
    heads = probes.shape[0]
    wide = jnp.concatenate([probes] * heads, axis=1)
    own = iota(wide.shape, 1) // HEAD == iota(wide.shape, 0)
    probes = jnp.concatenate(bf16_parts(jnp.where(own, wide, 0.0), 3), axis=0).astype(BF16)

    def against(block):
        product = lax.dot_general(probes, block, CONTRACT_LANES, preferred_element_type=F32)
        return product[:heads] + (product[heads : 2 * heads] + product[2 * heads :])

    up_probe[...] = against(up[...])
    high, low = bf16_parts(against(weight[...]), 2)
    select = iota((SUBLANES, RANK), 0) == iota((SUBLANES, RANK), 1)
    downs = jnp.dot(jnp.where(select, 1.0, 0.0).astype(BF16), down[...], preferred_element_type=F32)
    for i in range(devices):
        block = jnp.concatenate([high, low, downs[:, i * rows : (i + 1) * rows]], axis=0)
        out[i] = block.astype(BF16)


def norm_kernel(states, gain, down, normed, low):
    values = states[...].astype(F32)
    scale = lax.rsqrt(jnp.mean(values * values, axis=-1, keepdims=True) + 1e-06)
    normed[...] = (values * scale * gain[...]).astype(BF16)
    low[...] = lax.dot_general(down[...], normed[...], CONTRACT_LANES, preferred_element_type=F32)


def reward_kernel(place, normed, low, received, up_probe, up, out):
    received = received[...].astype(F32)
    members = received.shape[0]
    heads = 2 * KV_HEADS
    probe = jnp.concatenate([received[i, : 2 * heads] for i in range(members)], axis=1).astype(BF16)
    score = lax.dot_general(probe, normed[...], CONTRACT_LANES, preferred_element_type=F32)
    score = score[:heads] + score[heads:]
    extra = up_probe[:, 0:1] * low[0:1, :]
    for i in range(1, RANK):
        extra = extra + up_probe[:, i : i + 1] * low[i : i + 1, :]
    score = (score + 0.0025 * extra) * (1.0 / math.sqrt(HEAD))
    terms = jnp.tanh(score[:KV_HEADS]) * score[KV_HEADS:]
    reward = sum_all(terms) * (1.0 / terms.shape[1])

    targets = out.shape[0]
    tile = (SUBLANES, LANES)
    lane = iota(tile, 1)
    row = jnp.where(lane == place[0] + 3 * targets, place[2].astype(F32), 0.0)
    for i, part in enumerate(bf16_parts(reward, 3)):
        row = row + jnp.where(lane == place[0] + i * targets, part, 0.0)
    row = jnp.where(iota(tile, 0) == RANK, row, 0.0)

    down = received[:, 2 * heads :]
    down = down.reshape(members // 2, 2, SUBLANES, down.shape[2])
    down = pair_upper(down[:, 0], down[:, 1]).reshape(members * RANK, down.shape[3])
    half = members * RANK // 2
    column_parts = up.shape[1] // LANES
    row_parts = targets // column_parts
    share = down.shape[1] // row_parts
    spare = jnp.zeros((half, LANES // 2 - share), F32)
    select = iota((SUBLANES, RANK), 0) == iota((SUBLANES, RANK), 1)
    ups = jnp.dot(jnp.where(select, 1.0, 0.0).astype(BF16), up[...], preferred_element_type=F32)
    for i in range(row_parts):
        mine = down[:, i * share : (i + 1) * share]
        mine = jnp.concatenate([mine[:half], spare, mine[half:], spare], axis=1)
        for j in range(column_parts):
            last = ups[:, j * LANES : (j + 1) * LANES] + row
            out[i * column_parts + j] = jnp.concatenate([mine, last], axis=0).astype(BF16)


def relay_kernel(received, out):
    last = received[...].astype(F32)
    last = last[:, last.shape[1] - SUBLANES :]
    row = jnp.sum(last, axis=0)
    last = last.reshape(last.shape[0] // 2, 2, SUBLANES, LANES)
    ups = pair_upper(last[:, 0], last[:, 1])
    block = jnp.concatenate([ups.reshape(-1, LANES), row], axis=0).astype(BF16)
    out[...] = jnp.broadcast_to(block[None], out.shape)


def order_kernel(received, out):
    sources, rows, _ = received.shape
    tiles = rows // SUBLANES - 1
    down = received[...].astype(F32)[:, : tiles * SUBLANES]
    down = down.reshape(sources // 2, 2, tiles, SUBLANES, LANES)
    upper = pair_upper(down[:, 0], down[:, 1])
    lower = pair_lower(down[:, 0], down[:, 1])
    for i in range(tiles):
        out[2 * i] = upper[:, i].reshape(-1, LANES).astype(BF16)
        out[2 * i + 1] = lower[:, i].reshape(-1, LANES).astype(BF16)


def update_kernel(place, received, down, fitness, out):
    members, rows, _ = received.shape
    received = received[...].astype(F32)
    count = rows - SUBLANES
    sources = count // RANK
    total = members * sources
    tile = iota((members, SUBLANES, LANES), 1) == RANK
    table = jnp.sum(jnp.where(tile, received[:, count:], 0.0), axis=1)
    lane = iota(table.shape, 1)
    valid = lane < sources
    second = pltpu.roll(table, LANES - sources, axis=1)
    third = pltpu.roll(table, LANES - 2 * sources, axis=1)
    reward = jnp.where(valid, table + (second + third), 0.0)
    group = jnp.where(valid, pltpu.roll(table, LANES - 3 * sources, axis=1), -1.0)
    sums = [
        jnp.sum(jnp.where(group == float(i), reward, 0.0), axis=0, keepdims=True)
        for i in range(total // GROUP_MEMBERS)
    ]
    sums = jnp.sum(jnp.concatenate(sums, axis=0), axis=1, keepdims=True) * (1.0 / GROUP_MEMBERS)
    baseline = jnp.zeros_like(reward)
    for i in range(total // GROUP_MEMBERS):
        baseline = jnp.where(group == float(i), sums[i : i + 1, :], baseline)
    centered = jnp.where(valid, reward - baseline, 0.0)
    spread = sum_all(centered * centered) * (1.0 / total)
    shaped = centered / jnp.sqrt(spread + 1e-05)
    own = jnp.where((iota(table.shape, 0) == place[1]) & (lane == place[0]), shaped, 0.0)
    fitness[...] = sum_all(own)

    chosen = iota((count, LANES), 1) == iota((count, LANES), 0) // RANK
    weights = jnp.where(chosen[None], jnp.broadcast_to(shaped[:, None, :], (members, count, LANES)), 0.0)
    weighted = received[:, :count] * jnp.sum(weights, axis=2, keepdims=True)
    high = weighted.astype(BF16)
    low = (weighted - high.astype(F32)).astype(BF16)
    half = members // 2
    flat = half * count
    columns = [block[start : start + half].reshape(flat, LANES) for start in (0, half) for block in (high, low)]
    columns = jnp.concatenate(columns, axis=1)
    downs = down[...].reshape(flat, LANES)
    product = lax.dot_general(downs, columns, CONTRACT_ROWS, preferred_element_type=F32)
    middle = LANES // 2
    first = product[:middle, :LANES] + product[:middle, LANES : 2 * LANES]
    second = product[middle:, 2 * LANES : 3 * LANES] + product[middle:, 3 * LANES :]
    block = ((first + second) * (1.0 / math.sqrt(RANK * total)))[: out.shape[1]]
    out[...] = jnp.broadcast_to(block.astype(BF16)[None], out.shape)


def assemble_kernel(blocks, out):
    sources, share, _ = blocks.shape
    column_parts = out.shape[1] // LANES
    for i in range(sources):
        row, column = i // column_parts * share, i % column_parts * LANES
        out[row : row + share, column : column + LANES] = blocks[i].astype(F32)


def call(kernel, out_shape, in_specs, *operands, scratch=(), vmem=40):
    many = isinstance(out_shape, (list, tuple))
    return pl.pallas_call(
        kernel,
        out_shape=out_shape,
        in_specs=in_specs,
        out_specs=[VMEM] * len(out_shape) if many else VMEM,
        scratch_shapes=scratch,
        compiler_params=pltpu.CompilerParams(vmem_limit_bytes=vmem * 1024 * 1024),
    )(*operands)


def exchange(array, axes):
    return lax.all_to_all(array, axes, split_axis=0, concat_axis=0, tiled=True)


def local(
    prompt_states,
    norm_gain,
    kv_weight,
    probe_keys,
    probe_values,
    down_factors,
    up_factors,
    group_ids,
):
    pop = lax.axis_size(XY)
    mp = lax.axis_size(ZC)
    place = jnp.stack([lax.axis_index(XY), lax.axis_index(ZC), group_ids[0]]).astype(jnp.int32)
    states, down, up = prompt_states[0], down_factors[0], up_factors[0]
    tokens, width = states.shape
    columns = up.shape[1]
    rows = width // mp
    share = rows * columns // (pop * LANES)
    heads = 2 * KV_HEADS
    operands = (kv_weight, probe_keys, probe_values, up, down)
    up_probe, parts = call(
        probe_kernel,
        [
            jax.ShapeDtypeStruct((heads, RANK), F32),
            jax.ShapeDtypeStruct((mp, 3 * heads, rows), BF16),
        ],
        [pl.BlockSpec(memory_space=pltpu.HBM)] * len(operands),
        *operands,
        scratch=[pltpu.VMEM(a.shape, a.dtype) for a in operands] + [pltpu.SemaphoreType.DMA((len(operands),))],
        vmem=60,
    )
    parts = exchange(parts, ZC)
    normed, low = call(
        norm_kernel,
        [jax.ShapeDtypeStruct((tokens, width), BF16), jax.ShapeDtypeStruct((RANK, tokens), F32)],
        [VMEM] * 3,
        states,
        norm_gain[None],
        down,
    )
    half = mp * RANK // 2
    pieces = call(
        reward_kernel,
        jax.ShapeDtypeStruct((pop, half + SUBLANES, LANES), BF16),
        [SMEM] + [VMEM] * 5,
        place,
        normed,
        low,
        parts,
        up_probe,
        up,
    )
    pieces = exchange(pieces, XY)
    ups = call(relay_kernel, jax.ShapeDtypeStruct((mp, pop * RANK + SUBLANES, LANES), BF16), [VMEM], pieces)
    ups = exchange(ups, ZC)
    downs = call(order_kernel, jax.ShapeDtypeStruct((mp // 2, pop * RANK, LANES), BF16), [VMEM], pieces)
    fitness, blocks = call(
        update_kernel,
        [jax.ShapeDtypeStruct((1, 1), F32), jax.ShapeDtypeStruct((pop, share, LANES), BF16)],
        [SMEM, VMEM, VMEM],
        place,
        ups,
        downs,
    )
    blocks = exchange(blocks, XY)
    update = call(assemble_kernel, jax.ShapeDtypeStruct((rows, columns), F32), [VMEM], blocks)
    return (fitness.reshape(1), update)


def solution(mesh):
    grid = Mesh(mesh.devices.reshape(4, 8, 8, 2), ALL)
    in_specs = (
        P(ALL, None, None),
        P(),
        P(ZC, None),
        P(),
        P(),
        P(ALL, None, None),
        P(ALL, None, None),
        P(ALL),
    )
    out_specs = (P(ALL), P(ZC, None))
    return jax.shard_map(local, mesh=grid, in_specs=in_specs, out_specs=out_specs, check_vma=False)
```

time: 124 us -> 95.2 us (0.77)
  blocking collectives: 60.3 us -> 46 us
  starting transfers between devices: 24.1 us -> 14 us
  local copies, waits for them, and re-layouts: 6.79 us -> 2.98 us
    all_to_all x3 -> x2, blocking collectives: 60.3 us -> 46 us  [exchange(): return lax.all_to_all(array, axes, split_axis=0, concat_axis=0, tiled=True)]
    all_to_all x3 -> x2, starting transfers between devices: 24.1 us -> 14 us  [exchange(): return lax.all_to_all(array, axes, split_axis=0, concat_axis=0, tiled=True)]
    unnamed x14 -> x8, local copies, waits for them, and re-layouts: 6.06 us -> 2.25 us
    all_to_all x3 -> x2, waiting for transfers between devices: 22.5 us -> 21.7 us  [exchange(): return lax.all_to_all(array, axes, split_axis=0, concat_axis=0, tiled=True)]
  transfers between devices with their start and end apart: 3 -> 2, of which waited for: 3 -> 2; matrix products, arithmetic and copies ran while one was open for 1% -> 1% of each run, Pallas kernels for 2% -> 1%
where the time goes in v2:
time: 95.2 us; the launch traced here: 94.1 us
  blocking collectives  46 us (48%)
  waiting for transfers between devices  21.7 us (23%)
  starting transfers between devices  14 us (15%)
  Pallas kernels  8.07 us (8%)
  local copies, waits for them, and re-layouts  2.98 us (3%)
  between operations  1.37 us (1%)
    all_to_all x2, blocking collectives, exchange(): return lax.all_to_all(array, axes, split_axis=0, concat_axis=0, tiled=True)  46 us
    all_to_all x2, waiting for transfers between devices, exchange(): return lax.all_to_all(array, axes, split_axis=0, concat_axis=0, tiled=True)  21.7 us
    all_to_all x2, starting transfers between devices, exchange(): return lax.all_to_all(array, axes, split_axis=0, concat_axis=0, tiled=True)  14 us
    pallas_call x7, Pallas kernels, call(): pl.pallas_call(kernel, out_shape=out_shape, in_specs=in_specs, out_specs=...  8.07 us
    unnamed x8, local copies, waits for them, and re-layouts  2.25 us
  transfers between devices with their start and end apart: 2, of which 2 were waited for; matrix products, arithmetic and copies ran while one was open for 1% of the time, Pallas kernels for 1%

profile of v2, /device:TPU:8, one launch (start us, length us, event | category | flops | bytes accessed | tf_op | source)
XLA Modules:
  0.0 94.1 jit_solution(4661740721072386791)
XLA Ops:
  0.6 0.0 copy-start.2
  0.6 2.1 %shard_map.96 = (f32[8,4]{1,0:T(8,128)}, bf16[16,24,224]{2,1,0:T(8,128)(2,1)}) custom-call(bf16[224,1024]{1,0:T(8,128)(2,1)} %weight_hbm.1, f32[4,128]{1,0:T(4,128)} %keys_hbm.1, f32[4,128]{1,0:T(4,128)} %values_hbm.1, bf16[4,1024]{1,0:T(4,128)(2,1)} %bitcast.9, bf16[4,3584]{1,0:T(4,128)(2,1)} %bitcast.7), custom_call_target="tpu_custom_call" | custom-call | tf_op jit(solution)/shard_map/pallas_call | solution.py:207
  2.7 0.0 copy-start.3
  2.8 10.4 %all-to-all-start = ((bf16[16,24,224]{2,1,0:T(8,128)(2,1)}), bf16[16,24,224]{2,1,0:T(8,128)(2,1)S(1)}, u32[]{:S(2)}, u32[]{:S(2)}) async-start(bf16[16,24,224]{2,1,0:T(8,128)(2,1)} %get-tuple-element.10), calls=%async_computation | async-start | bytes 393216 | tf_op jit(solution)/shard_map/all_to_all | solution.py:218
  13.9 0.7 broadcast_in_dim.3.gain
  14.6 0.0 copy-start
  14.6 1.5 %copy-done = bf16[1,256,3584]{2,1,0:T(8,128)(2,1)S(1)} copy-done((bf16[1,256,3584]{2,1,0:T(8,128)(2,1)S(1)}, bf16[1,256,3584]{2,1,0:T(8,128)(2,1)}, u32[]{:S(2)}) %copy-start) | copy-done | bytes 1835032
  16.1 0.0 copy-start.1
  16.1 0.7 copy-done.1
  16.9 1.0 %shard_map.95 = (bf16[256,3584]{1,0:T(8,128)(2,1)S(1)}, f32[4,256]{1,0:T(4,128)S(1)}) custom-call(bf16[256,3584]{1,0:T(8,128)(2,1)S(1)} %bitcast.6, f32[1,3584]{1,0:T(1,128)S(1)} %broadcast_in_dim.3.gain, bf16[4,3584]{1,0:T(4,128)(2,1)S(1)} %bitcast.8), custom_call_target="tpu_custom_call" | custom-call | tf_op jit(solution)/shard_map/pallas_call | solution.py:207
  17.9 0.1 pad_add_fusion.place
  18.0 5.2 %all-to-all-done.received = bf16[16,24,224]{2,1,0:T(8,128)(2,1)S(1)} async-done(((bf16[16,24,224]{2,1,0:T(8,128)(2,1)}), bf16[16,24,224]{2,1,0:T(8,128)(2,1)S(1)}, u32[]{:S(2)}, u32[]{:S(2)}) %all-to-all-start) | async-done | bytes 172064 | tf_op jit(solution)/shard_map/all_to_all | solution.py:218
  23.2 0.0 copy-done.2
  23.2 0.0 copy-done.3
  23.2 1.2 %shard_map.97 = bf16[32,40,128]{2,1,0:T(8,128)(2,1)S(1)} custom-call(s32[3]{0:T(128)S(1)} %pad_add_fusion.place, bf16[256,3584]{1,0:T(8,128)(2,1)S(1)} %get-tuple-element.8.normed, f32[4,256]{1,0:T(4,128)S(1)} %get-tuple-element.9.low, bf16[16,24,224]{2,1,0:T(8,128)(2,1)S(1)} %all-to-all-done.received, f32[8,4]{1,0:T(8,128)S(1)} %copy-done.3, ...), custom_call_target="tpu_custom_call" | custom-call | tf_op jit(solution)/shard_map/pallas_call | solution.py:207
  24.4 24.4 %all_to_all.20.received = bf16[32,40,128]{2,1,0:T(8,128)(2,1)S(1)} all-to-all(bf16[32,40,128]{2,1,0:T(8,128)(2,1)S(1)} %shard_map.97), channel_id=1, replica_groups=mesh['x'=4,'y'=8,'z'=8,'core'=2] {'x','y'}, dimensions={0} | all-to-all | bytes 655360 | tf_op jit(solution)/shard_map/all_to_all | solution.py:218
  48.9 0.8 shard_map.98
  49.7 3.6 %all-to-all-start.2 = ((bf16[16,136,128]{2,1,0:T(8,128)(2,1)}), bf16[16,136,128]{2,1,0:T(8,128)(2,1)S(1)}, u32[]{:S(2)}, u32[]{:S(2)}) async-start(bf16[16,136,128]{2,1,0:T(8,128)(2,1)} %shard_map.98), calls=%async_computation.2 | async-start | bytes 1114112 | tf_op jit(solution)/shard_map/all_to_all | solution.py:218
  53.3 0.1 shard_map.99.down
  53.4 16.5 %all-to-all-done.2.received = bf16[16,136,128]{2,1,0:T(8,128)(2,1)S(1)} async-done(((bf16[16,136,128]{2,1,0:T(8,128)(2,1)}), bf16[16,136,128]{2,1,0:T(8,128)(2,1)S(1)}, u32[]{:S(2)}, u32[]{:S(2)}) %all-to-all-start.2) | async-done | bytes 557088 | tf_op jit(solution)/shard_map/all_to_all | solution.py:218
  69.8 1.8 %shard_map.100 = (f32[1,1]{1,0:T(1,128)}, bf16[32,56,128]{2,1,0:T(8,128)(2,1)S(1)}) custom-call(s32[3]{0:T(128)S(1)} %pad_add_fusion.place, bf16[16,136,128]{2,1,0:T(8,128)(2,1)S(1)} %all-to-all-done.2.received, bf16[8,128,128]{2,1,0:T(8,128)(2,1)S(1)} %shard_map.99.down), custom_call_target="tpu_custom_call" | custom-call | tf_op jit(solution)/shard_map/pallas_call | solution.py:207
  71.6 21.5 %all_to_all.21.blocks = bf16[32,56,128]{2,1,0:T(8,128)(2,1)S(1)} all-to-all(bf16[32,56,128]{2,1,0:T(8,128)(2,1)S(1)} %get-tuple-element.13), channel_id=1, replica_groups=mesh['x'=4,'y'=8,'z'=8,'core'=2] {'x','y'}, dimensions={0} | all-to-all | bytes 917504 | tf_op jit(solution)/shard_map/all_to_all | solution.py:218
  93.2 1.0 %shard_map.101 = f32[224,1024]{1,0:T(8,128)} custom-call(bf16[32,56,128]{2,1,0:T(8,128)(2,1)S(1)} %all_to_all.21.blocks), custom_call_target="tpu_custom_call" | custom-call | tf_op jit(solution)/shard_map/pallas_call | solution.py:207
Async XLA Ops:
  0.6 22.5 %copy-start.2 = (bf16[1,4,1024]{2,1,0:T(4,128)(2,1)S(1)}, bf16[1,4,1024]{2,1,0:T(4,128)(2,1)}, u32[]{:S(2)}) copy-start(bf16[1,4,1024]{2,1,0:T(4,128)(2,1)} %param.14) | copy-start | bytes 24580
  2.7 20.4 %copy-start.3 = (f32[8,4]{1,0:T(8,128)S(1)}, f32[8,4]{1,0:T(8,128)}, u32[]{:S(2)}) copy-start(f32[8,4]{1,0:T(8,128)} %get-tuple-element.11.up_probe) | copy-start | bytes 388
  2.8 20.4 %all-to-all-start = ((bf16[16,24,224]{2,1,0:T(8,128)(2,1)}), bf16[16,24,224]{2,1,0:T(8,128)(2,1)S(1)}, u32[]{:S(2)}, u32[]{:S(2)}) async-start(bf16[16,24,224]{2,1,0:T(8,128)(2,1)} %get-tuple-element.10), calls=%async_computation | async-start | bytes 393216 | tf_op jit(solution)/shard_map/all_to_all | solution.py:218
  14.6 1.5 %copy-start = (bf16[1,256,3584]{2,1,0:T(8,128)(2,1)S(1)}, bf16[1,256,3584]{2,1,0:T(8,128)(2,1)}, u32[]{:S(2)}) copy-start(bf16[1,256,3584]{2,1,0:T(8,128)(2,1)} %param.8) | copy-start | bytes 5505028
  16.1 0.7 copy-start.1
  49.7 20.1 %all-to-all-start.2 = ((bf16[16,136,128]{2,1,0:T(8,128)(2,1)}), bf16[16,136,128]{2,1,0:T(8,128)(2,1)S(1)}, u32[]{:S(2)}, u32[]{:S(2)}) async-start(bf16[16,136,128]{2,1,0:T(8,128)(2,1)} %shard_map.98), calls=%async_computation.2 | async-start | bytes 1114112 | tf_op jit(solution)/shard_map/all_to_all | solution.py:218

commit v3 on v2

--- a/solution.py
+++ b/solution.py
@@ -22,7 +22,6 @@
 F32 = jnp.float32
 BF16 = jnp.bfloat16
 CONTRACT_LANES = (((1,), (1,)), ((), ()))
-CONTRACT_ROWS = (((0,), (0,)), ((), ()))
 
 
 def bf16_parts(value, count):
@@ -50,33 +49,48 @@
     return jnp.where(iota(even.shape, even.ndim - 2) < RANK, pltpu.roll(even, RANK, axis=even.ndim - 2), odd)
 
 
+def probe_rows(probe_keys, probe_values):
+    probes = jnp.concatenate([probe_keys[...], probe_values[...]], axis=0)
+    wide = jnp.concatenate([probes] * probes.shape[0], axis=1)
+    own = iota(wide.shape, 1) // HEAD == iota(wide.shape, 0)
+    return jnp.concatenate(bf16_parts(jnp.where(own, wide, 0.0), 3), axis=0).astype(BF16)
+
+
+def against_probes(block, probes):
+    product = lax.dot_general(probes, block, CONTRACT_LANES, preferred_element_type=F32)
+    heads = product.shape[0] // 3
+    return product[:heads] + (product[heads : 2 * heads] + product[2 * heads :])
+
+
+def placed(block, offset):
+    shape = (SUBLANES, RANK)
+    select = jnp.where(iota(shape, 0) == iota(shape, 1) + offset, 1.0, 0.0).astype(BF16)
+    return jnp.dot(select, block, preferred_element_type=F32)
+
+
 def probe_kernel(weight_hbm, keys_hbm, values_hbm, up_hbm, down_hbm, up_probe, out, *scratch):
     buffers, sems = scratch[:5], scratch[5]
     sources = (weight_hbm, keys_hbm, values_hbm, up_hbm, down_hbm)
     copies = [pltpu.make_async_copy(a, b, sems.at[i]) for i, (a, b) in enumerate(zip(sources, buffers))]
     for copy in copies:
         copy.start()
-    for copy in copies:
+    weight, probe_keys, probe_values, up, down = buffers
+    for copy in copies[1:]:
         copy.wait()
-    weight, probe_keys, probe_values, up, down = buffers
-    devices, _, rows = out.shape
-    probes = jnp.concatenate([probe_keys[...], probe_values[...]], axis=0)
-    heads = probes.shape[0]
-    wide = jnp.concatenate([probes] * heads, axis=1)
-    own = iota(wide.shape, 1) // HEAD == iota(wide.shape, 0)
-    probes = jnp.concatenate(bf16_parts(jnp.where(own, wide, 0.0), 3), axis=0).astype(BF16)
-
-    def against(block):
-        product = lax.dot_general(probes, block, CONTRACT_LANES, preferred_element_type=F32)
-        return product[:heads] + (product[heads : 2 * heads] + product[2 * heads :])
-
-    up_probe[...] = against(up[...])
-    high, low = bf16_parts(against(weight[...]), 2)
-    select = iota((SUBLANES, RANK), 0) == iota((SUBLANES, RANK), 1)
-    downs = jnp.dot(jnp.where(select, 1.0, 0.0).astype(BF16), down[...], preferred_element_type=F32)
+    probes = probe_rows(probe_keys, probe_values)
+    up_probe[...] = against_probes(up[...], probes)
+    devices = out.shape[0]
+    rows = weight.shape[0]
+    first = placed(down[...], 0)
+    second = jnp.concatenate([placed(down[...], RANK), jnp.zeros((SUBLANES, LANES), F32)], axis=1)
+    copies[0].wait()
+    product = jnp.concatenate(bf16_parts(against_probes(weight[...], probes), 2), axis=0)
+    spare = jnp.zeros((product.shape[0], 2 * LANES - rows), F32)
+    product = jnp.concatenate([product[:, :LANES], jnp.concatenate([product[:, LANES:], spare], axis=1)], axis=0)
     for i in range(devices):
-        block = jnp.concatenate([high, low, downs[:, i * rows : (i + 1) * rows]], axis=0)
-        out[i] = block.astype(BF16)
+        start = i * rows
+        block = first[:, start : start + LANES] + second[:, start + LANES : start + 2 * LANES]
+        out[i] = jnp.concatenate([product, block], axis=0).astype(BF16)
 
 
 def norm_kernel(states, gain, down, normed, low):
@@ -90,7 +104,11 @@
     received = received[...].astype(F32)
     members = received.shape[0]
     heads = 2 * KV_HEADS
-    probe = jnp.concatenate([received[i, : 2 * heads] for i in range(members)], axis=1).astype(BF16)
+    rest = normed.shape[1] // members - LANES
+    probe = []
+    for i in range(members):
+        probe += [received[i, : 2 * heads], received[i, 2 * heads : 4 * heads, :rest]]
+    probe = jnp.concatenate(probe, axis=1).astype(BF16)
     score = lax.dot_general(probe, normed[...], CONTRACT_LANES, preferred_element_type=F32)
     score = score[:heads] + score[heads:]
     extra = up_probe[:, 0:1] * low[0:1, :]
@@ -108,16 +126,16 @@
         row = row + jnp.where(lane == place[0] + i * targets, part, 0.0)
     row = jnp.where(iota(tile, 0) == RANK, row, 0.0)
 
-    down = received[:, 2 * heads :]
-    down = down.reshape(members // 2, 2, SUBLANES, down.shape[2])
-    down = pair_upper(down[:, 0], down[:, 1]).reshape(members * RANK, down.shape[3])
+    down = received[:, 4 * heads :].reshape(members // 2, 2, SUBLANES, LANES)
+    first = pair_upper(down[:, 0], down[:, 1]).reshape(members * RANK, LANES)
+    second = pair_lower(down[:, 0], down[:, 1]).reshape(members * RANK, LANES)
+    down = jnp.concatenate([first, second[:, :rest]], axis=1)
     half = members * RANK // 2
     column_parts = up.shape[1] // LANES
     row_parts = targets // column_parts
     share = down.shape[1] // row_parts
     spare = jnp.zeros((half, LANES // 2 - share), F32)
-    select = iota((SUBLANES, RANK), 0) == iota((SUBLANES, RANK), 1)
-    ups = jnp.dot(jnp.where(select, 1.0, 0.0).astype(BF16), up[...], preferred_element_type=F32)
+    ups = placed(up[...], 0)
     for i in range(row_parts):
         mine = down[:, i * share : (i + 1) * share]
         mine = jnp.concatenate([mine[:half], spare, mine[half:], spare], axis=1)
@@ -143,14 +161,17 @@
     down = down.reshape(sources // 2, 2, tiles, SUBLANES, LANES)
     upper = pair_upper(down[:, 0], down[:, 1])
     lower = pair_lower(down[:, 0], down[:, 1])
-    for i in range(tiles):
-        out[2 * i] = upper[:, i].reshape(-1, LANES).astype(BF16)
-        out[2 * i + 1] = lower[:, i].reshape(-1, LANES).astype(BF16)
-
-
-def update_kernel(place, received, down, fitness, out):
-    members, rows, _ = received.shape
-    received = received[...].astype(F32)
+    ordered = [half[:, i].reshape(-1, LANES) for i in range(tiles) for half in (upper, lower)]
+    out[...] = jnp.transpose(jnp.concatenate(ordered, axis=0)).astype(BF16)
+
+
+def update_kernel(place, own, other, down, fitness, out):
+    chips, rows, _ = own.shape
+    members = 2 * chips
+    own, other = own[...].astype(F32), other[...].astype(F32)
+    first_core = place[1] % 2 == 0
+    cores = [jnp.where(first_core, own, other), jnp.where(first_core, other, own)]
+    received = jnp.stack(cores, axis=1).reshape(members, rows, LANES)
     count = rows - SUBLANES
     sources = count // RANK
     total = members * sources
@@ -173,8 +194,8 @@
     centered = jnp.where(valid, reward - baseline, 0.0)
     spread = sum_all(centered * centered) * (1.0 / total)
     shaped = centered / jnp.sqrt(spread + 1e-05)
-    own = jnp.where((iota(table.shape, 0) == place[1]) & (lane == place[0]), shaped, 0.0)
-    fitness[...] = sum_all(own)
+    mine = jnp.where((iota(table.shape, 0) == place[1]) & (lane == place[0]), shaped, 0.0)
+    fitness[...] = sum_all(mine)
 
     chosen = iota((count, LANES), 1) == iota((count, LANES), 0) // RANK
     weights = jnp.where(chosen[None], jnp.broadcast_to(shaped[:, None, :], (members, count, LANES)), 0.0)
@@ -185,8 +206,7 @@
     flat = half * count
     columns = [block[start : start + half].reshape(flat, LANES) for start in (0, half) for block in (high, low)]
     columns = jnp.concatenate(columns, axis=1)
-    downs = down[...].reshape(flat, LANES)
-    product = lax.dot_general(downs, columns, CONTRACT_ROWS, preferred_element_type=F32)
+    product = jnp.dot(down[...], columns, preferred_element_type=F32)
     middle = LANES // 2
     first = product[:middle, :LANES] + product[:middle, LANES : 2 * LANES]
     second = product[middle:, 2 * LANES : 3 * LANES] + product[middle:, 3 * LANES :]
@@ -194,21 +214,27 @@
     out[...] = jnp.broadcast_to(block.astype(BF16)[None], out.shape)
 
 
-def assemble_kernel(blocks, out):
+def assemble_kernel(blocks, out_hbm, out, sems):
     sources, share, _ = blocks.shape
     column_parts = out.shape[1] // LANES
-    for i in range(sources):
-        row, column = i // column_parts * share, i % column_parts * LANES
-        out[row : row + share, column : column + LANES] = blocks[i].astype(F32)
-
-
-def call(kernel, out_shape, in_specs, *operands, scratch=(), vmem=40):
+    copies = []
+    for i in range(sources // column_parts):
+        rows = pl.ds(i * share, share)
+        for j in range(column_parts):
+            out[rows, j * LANES : (j + 1) * LANES] = blocks[i * column_parts + j].astype(F32)
+        copies.append(pltpu.make_async_copy(out.at[rows], out_hbm.at[rows], sems.at[i]))
+        copies[-1].start()
+    for copy in copies:
+        copy.wait()
+
+
+def call(kernel, out_shape, in_specs, *operands, scratch=(), vmem=40, out_spec=VMEM):
     many = isinstance(out_shape, (list, tuple))
     return pl.pallas_call(
         kernel,
         out_shape=out_shape,
         in_specs=in_specs,
-        out_specs=[VMEM] * len(out_shape) if many else VMEM,
+        out_specs=[out_spec] * len(out_shape) if many else out_spec,
         scratch_shapes=scratch,
         compiler_params=pltpu.CompilerParams(vmem_limit_bytes=vmem * 1024 * 1024),
     )(*operands)
@@ -242,7 +268,7 @@
         probe_kernel,
         [
             jax.ShapeDtypeStruct((heads, RANK), F32),
-            jax.ShapeDtypeStruct((mp, 3 * heads, rows), BF16),
+            jax.ShapeDtypeStruct((mp, 5 * heads, LANES), BF16),
         ],
         [pl.BlockSpec(memory_space=pltpu.HBM)] * len(operands),
         *operands,
@@ -271,19 +297,28 @@
         up,
     )
     pieces = exchange(pieces, XY)
-    ups = call(relay_kernel, jax.ShapeDtypeStruct((mp, pop * RANK + SUBLANES, LANES), BF16), [VMEM], pieces)
-    ups = exchange(ups, ZC)
-    downs = call(order_kernel, jax.ShapeDtypeStruct((mp // 2, pop * RANK, LANES), BF16), [VMEM], pieces)
+    ups = call(relay_kernel, jax.ShapeDtypeStruct((mp // 2, pop * RANK + SUBLANES, LANES), BF16), [VMEM], pieces)
+    ups = exchange(ups, "z")
+    other_ups = lax.ppermute(ups, "core", [(0, 1), (1, 0)])
+    downs = call(order_kernel, jax.ShapeDtypeStruct((LANES, mp // 2 * pop * RANK), BF16), [VMEM], pieces)
     fitness, blocks = call(
         update_kernel,
         [jax.ShapeDtypeStruct((1, 1), F32), jax.ShapeDtypeStruct((pop, share, LANES), BF16)],
-        [SMEM, VMEM, VMEM],
+        [SMEM, VMEM, VMEM, VMEM],
         place,
         ups,
+        other_ups,
         downs,
     )
     blocks = exchange(blocks, XY)
-    update = call(assemble_kernel, jax.ShapeDtypeStruct((rows, columns), F32), [VMEM], blocks)
+    update = call(
+        assemble_kernel,
+        jax.ShapeDtypeStruct((rows, columns), F32),
+        [VMEM],
+        blocks,
+        scratch=[pltpu.VMEM((rows, columns), F32), pltpu.SemaphoreType.DMA((pop * LANES // columns,))],
+        out_spec=pl.BlockSpec(memory_space=pltpu.HBM),
+    )
     return (fitness.reshape(1), update)
 
 

time: 95.2 us -> 91.1 us (0.957)
  waiting for transfers between devices: 21.7 us -> 5.85 us
  blocking collectives: 46 us -> 60.5 us
  starting transfers between devices: 14 us -> 12.3 us
    all_to_all x2 -> x1, waiting for transfers between devices: 21.7 us -> 4.47 us  [exchange(): return lax.all_to_all(array, axes, split_axis=0, concat_axis=0, tiled=True)]
    all_to_all x2 -> x3, blocking collectives: 46 us -> 60.5 us  [exchange(): return lax.all_to_all(array, axes, split_axis=0, concat_axis=0, tiled=True)]
    all_to_all x2 -> x1, starting transfers between devices: 14 us -> 10.4 us  [exchange(): return lax.all_to_all(array, axes, split_axis=0, concat_axis=0, tiled=True)]
    ppermute x0 -> x1, starting transfers between devices: none -> 1.91 us  [local(): other_ups = lax.ppermute(ups, 'core', [(0, 1), (1, 0)])]
    ppermute x0 -> x1, waiting for transfers between devices: none -> 1.38 us  [local(): other_ups = lax.ppermute(ups, 'core', [(0, 1), (1, 0)])]
where the time goes in v3:
time: 91.1 us; the launch traced here: 90.6 us
  blocking collectives  60.5 us (66%)
  starting transfers between devices  12.3 us (14%)
  Pallas kernels  7.41 us (8%)
  waiting for transfers between devices  5.85 us (6%)
  local copies, waits for them, and re-layouts  2.98 us (3%)
  between operations  1.37 us (2%)
    all_to_all x3, blocking collectives, exchange(): return lax.all_to_all(array, axes, split_axis=0, concat_axis=0, tiled=True)  60.5 us
    all_to_all x1, starting transfers between devices, exchange(): return lax.all_to_all(array, axes, split_axis=0, concat_axis=0, tiled=True)  10.4 us
    pallas_call x7, Pallas kernels, call(): pl.pallas_call(kernel, out_shape=out_shape, in_specs=in_specs, out_specs=...  7.41 us
    all_to_all x1, waiting for transfers between devices, exchange(): return lax.all_to_all(array, axes, split_axis=0, concat_axis=0, tiled=True)  4.47 us
    unnamed x8, local copies, waits for them, and re-layouts  2.25 us
    ppermute x1, starting transfers between devices, local(): other_ups = lax.ppermute(ups, 'core', [(0, 1), (1, 0)])  1.91 us
  transfers between devices with their start and end apart: 2, of which 2 were waited for; matrix products, arithmetic and copies ran while one was open for 1% of the time, Pallas kernels for 1%

profile of v3, /device:TPU:8, one launch (start us, length us, event | category | flops | bytes accessed | tf_op | source)
XLA Modules:
  0.0 90.6 jit_solution(3753614622967346701)
XLA Ops:
  0.6 0.0 copy-start.2
  0.6 2.2 %shard_map.96 = (f32[8,4]{1,0:T(8,128)}, bf16[16,40,128]{2,1,0:T(8,128)(2,1)}) custom-call(bf16[224,1024]{1,0:T(8,128)(2,1)} %weight_hbm.1, f32[4,128]{1,0:T(4,128)} %keys_hbm.1, f32[4,128]{1,0:T(4,128)} %values_hbm.1, bf16[4,1024]{1,0:T(4,128)(2,1)} %bitcast.9, bf16[4,3584]{1,0:T(4,128)(2,1)} %bitcast.7), custom_call_target="tpu_custom_call" | custom-call | tf_op jit(solution)/shard_map/pallas_call | solution.py:233
  2.8 0.0 copy-start.3
  2.8 10.4 %all-to-all-start = ((bf16[16,40,128]{2,1,0:T(8,128)(2,1)}), bf16[16,40,128]{2,1,0:T(8,128)(2,1)S(1)}, u32[]{:S(2)}, u32[]{:S(2)}) async-start(bf16[16,40,128]{2,1,0:T(8,128)(2,1)} %get-tuple-element.10), calls=%async_computation | async-start | bytes 327680 | tf_op jit(solution)/shard_map/all_to_all | solution.py:244
  13.9 0.7 broadcast_in_dim.3.gain
  14.7 0.0 copy-start
  14.7 1.5 %copy-done = bf16[1,256,3584]{2,1,0:T(8,128)(2,1)S(1)} copy-done((bf16[1,256,3584]{2,1,0:T(8,128)(2,1)S(1)}, bf16[1,256,3584]{2,1,0:T(8,128)(2,1)}, u32[]{:S(2)}) %copy-start) | copy-done | bytes 1835032
  16.2 0.0 copy-start.1
  16.2 0.7 copy-done.1
  16.9 1.0 %shard_map.95 = (bf16[256,3584]{1,0:T(8,128)(2,1)S(1)}, f32[4,256]{1,0:T(4,128)S(1)}) custom-call(bf16[256,3584]{1,0:T(8,128)(2,1)S(1)} %bitcast.6, f32[1,3584]{1,0:T(1,128)S(1)} %broadcast_in_dim.3.gain, bf16[4,3584]{1,0:T(4,128)(2,1)S(1)} %bitcast.8), custom_call_target="tpu_custom_call" | custom-call | tf_op jit(solution)/shard_map/pallas_call | solution.py:233
  17.9 0.1 pad_add_fusion.place
  18.0 4.5 %all-to-all-done.received = bf16[16,40,128]{2,1,0:T(8,128)(2,1)S(1)} async-done(((bf16[16,40,128]{2,1,0:T(8,128)(2,1)}), bf16[16,40,128]{2,1,0:T(8,128)(2,1)S(1)}, u32[]{:S(2)}, u32[]{:S(2)}) %all-to-all-start) | async-done | bytes 163872 | tf_op jit(solution)/shard_map/all_to_all | solution.py:244
  22.5 0.0 copy-done.2
  22.5 0.0 copy-done.3
  22.5 1.2 %shard_map.97 = bf16[32,40,128]{2,1,0:T(8,128)(2,1)S(1)} custom-call(s32[3]{0:T(128)S(1)} %pad_add_fusion.place, bf16[256,3584]{1,0:T(8,128)(2,1)S(1)} %get-tuple-element.8.normed, f32[4,256]{1,0:T(4,128)S(1)} %get-tuple-element.9.low, bf16[16,40,128]{2,1,0:T(8,128)(2,1)S(1)} %all-to-all-done.received, f32[8,4]{1,0:T(8,128)S(1)} %copy-done.3, ...), custom_call_target="tpu_custom_call" | custom-call | tf_op jit(solution)/shard_map/pallas_call | solution.py:233
  23.8 24.4 %all_to_all.20.received = bf16[32,40,128]{2,1,0:T(8,128)(2,1)S(1)} all-to-all(bf16[32,40,128]{2,1,0:T(8,128)(2,1)S(1)} %shard_map.97), channel_id=1, replica_groups=mesh['x'=4,'y'=8,'z'=8,'core'=2] {'x','y'}, dimensions={0} | all-to-all | bytes 655360 | tf_op jit(solution)/shard_map/all_to_all | solution.py:244
  48.3 14.6 %all_to_all.21.own = bf16[8,136,128]{2,1,0:T(8,128)(2,1)S(1)} all-to-all(bf16[8,136,128]{2,1,0:T(8,128)(2,1)S(1)} %shard_map.98), channel_id=1, replica_groups=mesh['x'=4,'y'=8,'z'=8,'core'=2] {'z'}, dimensions={0} | all-to-all | bytes 557056 | tf_op jit(solution)/shard_map/all_to_all | solution.py:244
  62.8 1.9 %collective-permute-start = (bf16[8,136,128]{2,1,0:T(8,128)(2,1)S(1)}, bf16[8,136,128]{2,1,0:T(8,128)(2,1)S(1)}, u32[]{:S(2)}, u32[]{:S(2)}) collective-permute-start(bf16[8,136,128]{2,1,0:T(8,128)(2,1)S(1)} %all_to_all.21.own), channel_id=1, source_target_pairs={{0,1},{1,0},{2,3},{3,2},{4,5},{5,4},{6,7},{7,6},{8,9},{9,8},{10,11... | collective-permute-start | bytes 835592 | tf_op jit(solution)/shard_map/ppermute | solution.py:302
  64.7 0.1 shard_map.99.down
  64.9 1.4 %collective-permute-done.other = bf16[8,136,128]{2,1,0:T(8,128)(2,1)S(1)} collective-permute-done((bf16[8,136,128]{2,1,0:T(8,128)(2,1)S(1)}, bf16[8,136,128]{2,1,0:T(8,128)(2,1)S(1)}, u32[]{:S(2)}, u32[]{:S(2)}) %collective-permute-start) | collective-permute-done | bytes 278560 | tf_op jit(solution)/shard_map/ppermute | solution.py:302
  66.3 1.8 %shard_map.100 = (f32[1,1]{1,0:T(1,128)}, bf16[32,56,128]{2,1,0:T(8,128)(2,1)S(1)}) custom-call(s32[3]{0:T(128)S(1)} %pad_add_fusion.place, bf16[8,136,128]{2,1,0:T(8,128)(2,1)S(1)} %all_to_all.21.own, bf16[8,136,128]{2,1,0:T(8,128)(2,1)S(1)} %collective-permute-done.other, bf16[128,1024]{1,0:T(8,128)(2,1)S(1)} %shard_map.99.down), custom_call_target="tpu_custom_call" | custom-call | tf_op jit(solution)/shard_map/pallas_call | solution.py:233
  68.1 21.5 %all_to_all.22.blocks = bf16[32,56,128]{2,1,0:T(8,128)(2,1)S(1)} all-to-all(bf16[32,56,128]{2,1,0:T(8,128)(2,1)S(1)} %get-tuple-element.13), channel_id=1, replica_groups=mesh['x'=4,'y'=8,'z'=8,'core'=2] {'x','y'}, dimensions={0} | all-to-all | bytes 917504 | tf_op jit(solution)/shard_map/all_to_all | solution.py:244
  89.6 1.0 %shard_map.101 = f32[224,1024]{1,0:T(8,128)} custom-call(bf16[32,56,128]{2,1,0:T(8,128)(2,1)S(1)} %all_to_all.22.blocks), custom_call_target="tpu_custom_call" | custom-call | tf_op jit(solution)/shard_map/pallas_call | solution.py:233
  (1 shorter events, 0.0 us)
Async XLA Ops:
  0.6 21.9 %copy-start.2 = (bf16[1,4,1024]{2,1,0:T(4,128)(2,1)S(1)}, bf16[1,4,1024]{2,1,0:T(4,128)(2,1)}, u32[]{:S(2)}) copy-start(bf16[1,4,1024]{2,1,0:T(4,128)(2,1)} %param.14) | copy-start | bytes 24580
  2.8 19.7 %copy-start.3 = (f32[8,4]{1,0:T(8,128)S(1)}, f32[8,4]{1,0:T(8,128)}, u32[]{:S(2)}) copy-start(f32[8,4]{1,0:T(8,128)} %get-tuple-element.11.up_probe) | copy-start | bytes 388
  2.8 19.7 %all-to-all-start = ((bf16[16,40,128]{2,1,0:T(8,128)(2,1)}), bf16[16,40,128]{2,1,0:T(8,128)(2,1)S(1)}, u32[]{:S(2)}, u32[]{:S(2)}) async-start(bf16[16,40,128]{2,1,0:T(8,128)(2,1)} %get-tuple-element.10), calls=%async_computation | async-start | bytes 327680 | tf_op jit(solution)/shard_map/all_to_all | solution.py:244
  14.7 1.5 %copy-start = (bf16[1,256,3584]{2,1,0:T(8,128)(2,1)S(1)}, bf16[1,256,3584]{2,1,0:T(8,128)(2,1)}, u32[]{:S(2)}) copy-start(bf16[1,256,3584]{2,1,0:T(8,128)(2,1)} %param.8) | copy-start | bytes 5505028
  16.2 0.7 copy-start.1
  62.8 3.4 %collective-permute-start = (bf16[8,136,128]{2,1,0:T(8,128)(2,1)S(1)}, bf16[8,136,128]{2,1,0:T(8,128)(2,1)S(1)}, u32[]{:S(2)}, u32[]{:S(2)}) collective-permute-start(bf16[8,136,128]{2,1,0:T(8,128)(2,1)S(1)} %all_to_all.21.own), channel_id=1, source_target_pairs={{0,1},{1,0},{2,3},{3,2},{4,5},{5,4},{6,7},{7,6},{8,9},{9,8},{10,11... | collective-permute-start | bytes 835592 | tf_op jit(solution)/shard_map/ppermute | solution.py:302

commit v4 on v3

--- a/solution.py
+++ b/solution.py
@@ -14,7 +14,7 @@
 GROUP_MEMBERS = 16
 LANES = 128
 SUBLANES = 8
-XY = ("x", "y")
+XY = ("y", "x")
 ZC = ("z", "core")
 ALL = ("x", "y", "z", "core")
 VMEM = pl.BlockSpec(memory_space=pltpu.VMEM)
@@ -88,7 +88,7 @@
     spare = jnp.zeros((product.shape[0], 2 * LANES - rows), F32)
     product = jnp.concatenate([product[:, :LANES], jnp.concatenate([product[:, LANES:], spare], axis=1)], axis=0)
     for i in range(devices):
-        start = i * rows
+        start = (i % (devices // 2) * 2 + i // (devices // 2)) * rows
         block = first[:, start : start + LANES] + second[:, start + LANES : start + 2 * LANES]
         out[i] = jnp.concatenate([product, block], axis=0).astype(BF16)
 
@@ -107,7 +107,8 @@
     rest = normed.shape[1] // members - LANES
     probe = []
     for i in range(members):
-        probe += [received[i, : 2 * heads], received[i, 2 * heads : 4 * heads, :rest]]
+        source = received[i % 2 * (members // 2) + i // 2]
+        probe += [source[: 2 * heads], source[2 * heads : 4 * heads, :rest]]
     probe = jnp.concatenate(probe, axis=1).astype(BF16)
     score = lax.dot_general(probe, normed[...], CONTRACT_LANES, preferred_element_type=F32)
     score = score[:heads] + score[heads:]
@@ -126,9 +127,9 @@
         row = row + jnp.where(lane == place[0] + i * targets, part, 0.0)
     row = jnp.where(iota(tile, 0) == RANK, row, 0.0)
 
-    down = received[:, 4 * heads :].reshape(members // 2, 2, SUBLANES, LANES)
-    first = pair_upper(down[:, 0], down[:, 1]).reshape(members * RANK, LANES)
-    second = pair_lower(down[:, 0], down[:, 1]).reshape(members * RANK, LANES)
+    down = received[:, 4 * heads :].reshape(2, members // 2, SUBLANES, LANES)
+    first = pair_upper(down[0], down[1]).reshape(members * RANK, LANES)
+    second = pair_lower(down[0], down[1]).reshape(members * RANK, LANES)
     down = jnp.concatenate([first, second[:, :rest]], axis=1)
     half = members * RANK // 2
     column_parts = up.shape[1] // LANES
@@ -141,7 +142,7 @@
         mine = jnp.concatenate([mine[:half], spare, mine[half:], spare], axis=1)
         for j in range(column_parts):
             last = ups[:, j * LANES : (j + 1) * LANES] + row
-            out[i * column_parts + j] = jnp.concatenate([mine, last], axis=0).astype(BF16)
+            out[j * row_parts + i] = jnp.concatenate([mine, last], axis=0).astype(BF16)
 
 
 def relay_kernel(received, out):
@@ -159,24 +160,20 @@
     tiles = rows // SUBLANES - 1
     down = received[...].astype(F32)[:, : tiles * SUBLANES]
     down = down.reshape(sources // 2, 2, tiles, SUBLANES, LANES)
-    upper = pair_upper(down[:, 0], down[:, 1])
-    lower = pair_lower(down[:, 0], down[:, 1])
-    ordered = [half[:, i].reshape(-1, LANES) for i in range(tiles) for half in (upper, lower)]
-    out[...] = jnp.transpose(jnp.concatenate(ordered, axis=0)).astype(BF16)
+    for core, pair in enumerate((pair_upper, pair_lower)):
+        ordered = pair(down[:, 0], down[:, 1])
+        ordered = [ordered[:, i].reshape(-1, LANES) for i in range(tiles)]
+        out[core] = jnp.transpose(jnp.concatenate(ordered, axis=0)).astype(BF16)
 
 
 def update_kernel(place, own, other, down, fitness, out):
     chips, rows, _ = own.shape
-    members = 2 * chips
-    own, other = own[...].astype(F32), other[...].astype(F32)
-    first_core = place[1] % 2 == 0
-    cores = [jnp.where(first_core, own, other), jnp.where(first_core, other, own)]
-    received = jnp.stack(cores, axis=1).reshape(members, rows, LANES)
     count = rows - SUBLANES
     sources = count // RANK
-    total = members * sources
-    tile = iota((members, SUBLANES, LANES), 1) == RANK
-    table = jnp.sum(jnp.where(tile, received[:, count:], 0.0), axis=1)
+    total = 2 * chips * sources
+    tile = iota((chips, SUBLANES, LANES), 1) == RANK
+    table = [jnp.sum(jnp.where(tile, ref[...].astype(F32)[:, count:], 0.0), axis=1) for ref in (own, other)]
+    table = jnp.concatenate(table, axis=0)
     lane = iota(table.shape, 1)
     valid = lane < sources
     second = pltpu.roll(table, LANES - sources, axis=1)
@@ -194,22 +191,34 @@
     centered = jnp.where(valid, reward - baseline, 0.0)
     spread = sum_all(centered * centered) * (1.0 / total)
     shaped = centered / jnp.sqrt(spread + 1e-05)
-    mine = jnp.where((iota(table.shape, 0) == place[1]) & (lane == place[0]), shaped, 0.0)
-    fitness[...] = sum_all(mine)
-
-    chosen = iota((count, LANES), 1) == iota((count, LANES), 0) // RANK
-    weights = jnp.where(chosen[None], jnp.broadcast_to(shaped[:, None, :], (members, count, LANES)), 0.0)
-    weighted = received[:, :count] * jnp.sum(weights, axis=2, keepdims=True)
-    high = weighted.astype(BF16)
-    low = (weighted - high.astype(F32)).astype(BF16)
-    half = members // 2
+    mine = (iota(table.shape, 0) == place[1] // 2) & (lane == place[0])
+    fitness[...] = sum_all(jnp.where(mine, shaped, 0.0))
+
+    each = jnp.where(iota((LANES, count), 0) == iota((LANES, count), 1) // RANK, 1.0, 0.0).astype(BF16)
+    weights = jnp.concatenate(bf16_parts(shaped, 3), axis=0).astype(BF16)
+    weights = jnp.dot(weights, each, preferred_element_type=F32)
+    weights = weights[: 2 * chips] + (weights[2 * chips : 4 * chips] + weights[4 * chips :])
+    half = chips // 2
+    middle = LANES // 2
     flat = half * count
-    columns = [block[start : start + half].reshape(flat, LANES) for start in (0, half) for block in (high, low)]
-    columns = jnp.concatenate(columns, axis=1)
-    product = jnp.dot(down[...], columns, preferred_element_type=F32)
-    middle = LANES // 2
-    first = product[:middle, :LANES] + product[:middle, LANES : 2 * LANES]
-    second = product[middle:, 2 * LANES : 3 * LANES] + product[middle:, 3 * LANES :]
+    core = place[1] % 2
+    product = jnp.zeros((2 * LANES, 2 * LANES), F32)
+    for i, (which, ref) in enumerate(((core, own), (1 - core, other))):
+        scale = []
+        for j in range(half):
+            first = i * chips + j
+            rows_of = [jnp.broadcast_to(weights[k : k + 1], (middle, count)) for k in (first, first + half)]
+            scale.append(jnp.concatenate(rows_of, axis=0))
+        weighted = down[which].astype(F32) * jnp.concatenate(scale, axis=1)
+        high = weighted.astype(BF16)
+        low = (weighted - high.astype(F32)).astype(BF16)
+        ups = ref[...].astype(F32)[:, :count]
+        ups = [ups[start : start + half].reshape(flat, LANES) for start in (0, half)]
+        ups = jnp.concatenate(ups, axis=1).astype(BF16)
+        parts = jnp.concatenate([high, low], axis=0)
+        product = product + jnp.dot(parts, ups, preferred_element_type=F32)
+    first = product[:middle, :LANES] + product[LANES : LANES + middle, :LANES]
+    second = product[middle:LANES, LANES:] + product[LANES + middle :, LANES:]
     block = ((first + second) * (1.0 / math.sqrt(RANK * total)))[: out.shape[1]]
     out[...] = jnp.broadcast_to(block.astype(BF16)[None], out.shape)
 
@@ -217,11 +226,12 @@
 def assemble_kernel(blocks, out_hbm, out, sems):
     sources, share, _ = blocks.shape
     column_parts = out.shape[1] // LANES
+    row_parts = sources // column_parts
     copies = []
-    for i in range(sources // column_parts):
+    for i in range(row_parts):
         rows = pl.ds(i * share, share)
         for j in range(column_parts):
-            out[rows, j * LANES : (j + 1) * LANES] = blocks[i * column_parts + j].astype(F32)
+            out[rows, j * LANES : (j + 1) * LANES] = blocks[j * row_parts + i].astype(F32)
         copies.append(pltpu.make_async_copy(out.at[rows], out_hbm.at[rows], sems.at[i]))
         copies[-1].start()
     for copy in copies:
@@ -275,7 +285,7 @@
         scratch=[pltpu.VMEM(a.shape, a.dtype) for a in operands] + [pltpu.SemaphoreType.DMA((len(operands),))],
         vmem=60,
     )
-    parts = exchange(parts, ZC)
+    parts = exchange(parts, ("core", "z"))
     normed, low = call(
         norm_kernel,
         [jax.ShapeDtypeStruct((tokens, width), BF16), jax.ShapeDtypeStruct((RANK, tokens), F32)],
@@ -300,7 +310,7 @@
     ups = call(relay_kernel, jax.ShapeDtypeStruct((mp // 2, pop * RANK + SUBLANES, LANES), BF16), [VMEM], pieces)
     ups = exchange(ups, "z")
     other_ups = lax.ppermute(ups, "core", [(0, 1), (1, 0)])
-    downs = call(order_kernel, jax.ShapeDtypeStruct((LANES, mp // 2 * pop * RANK), BF16), [VMEM], pieces)
+    downs = call(order_kernel, jax.ShapeDtypeStruct((2, LANES, mp // 4 * pop * RANK), BF16), [VMEM], pieces)
     fitness, blocks = call(
         update_kernel,
         [jax.ShapeDtypeStruct((1, 1), F32), jax.ShapeDtypeStruct((pop, share, LANES), BF16)],

time: 91.1 us -> 89.1 us (0.978)
  blocking collectives: 60.5 us -> 59.3 us
    all_to_all x3, blocking collectives: 60.5 us -> 59.3 us  [exchange(): return lax.all_to_all(array, axes, split_axis=0, concat_axis=0, tiled=True)]
where the time goes in v4:
time: 89.1 us; the launch traced here: 88.6 us
  blocking collectives  59.3 us (67%)
  starting transfers between devices  12.3 us (14%)
  Pallas kernels  7.24 us (8%)
  waiting for transfers between devices  5.33 us (6%)
  local copies, waits for them, and re-layouts  2.98 us (3%)
  between operations  1.37 us (2%)
    all_to_all x3, blocking collectives, exchange(): return lax.all_to_all(array, axes, split_axis=0, concat_axis=0, tiled=True)  59.3 us
    all_to_all x1, starting transfers between devices, exchange(): return lax.all_to_all(array, axes, split_axis=0, concat_axis=0, tiled=True)  10.4 us
    pallas_call x7, Pallas kernels, call(): pl.pallas_call(kernel, out_shape=out_shape, in_specs=in_specs, out_specs=...  7.24 us
    all_to_all x1, waiting for transfers between devices, exchange(): return lax.all_to_all(array, axes, split_axis=0, concat_axis=0, tiled=True)  3.96 us
    unnamed x8, local copies, waits for them, and re-layouts  2.25 us
    ppermute x1, starting transfers between devices, local(): other_ups = lax.ppermute(ups, 'core', [(0, 1), (1, 0)])  1.91 us
  transfers between devices with their start and end apart: 2, of which 2 were waited for; matrix products, arithmetic and copies ran while one was open for 1% of the time, Pallas kernels for 1%

profile of v4, /device:TPU:8, one launch (start us, length us, event | category | flops | bytes accessed | tf_op | source)
XLA Modules:
  0.0 88.6 jit_solution(3385047531323014692)
XLA Ops:
  0.6 0.0 copy-start.2
  0.6 2.2 %shard_map.96 = (f32[8,4]{1,0:T(8,128)}, bf16[16,40,128]{2,1,0:T(8,128)(2,1)}) custom-call(bf16[224,1024]{1,0:T(8,128)(2,1)} %weight_hbm.1, f32[4,128]{1,0:T(4,128)} %keys_hbm.1, f32[4,128]{1,0:T(4,128)} %values_hbm.1, bf16[4,1024]{1,0:T(4,128)(2,1)} %bitcast.9, bf16[4,3584]{1,0:T(4,128)(2,1)} %bitcast.7), custom_call_target="tpu_custom_call" | custom-call | tf_op jit(solution)/shard_map/pallas_call | solution.py:243
  2.8 0.0 copy-start.3
  2.8 10.4 %all-to-all-start = ((bf16[16,40,128]{2,1,0:T(8,128)(2,1)}), bf16[16,40,128]{2,1,0:T(8,128)(2,1)S(1)}, u32[]{:S(2)}, u32[]{:S(2)}) async-start(bf16[16,40,128]{2,1,0:T(8,128)(2,1)} %get-tuple-element.10), calls=%async_computation | async-start | bytes 327680 | tf_op jit(solution)/shard_map/all_to_all | solution.py:254
  13.9 0.7 broadcast_in_dim.3.gain
  14.7 0.0 copy-start
  14.7 1.5 %copy-done = bf16[1,256,3584]{2,1,0:T(8,128)(2,1)S(1)} copy-done((bf16[1,256,3584]{2,1,0:T(8,128)(2,1)S(1)}, bf16[1,256,3584]{2,1,0:T(8,128)(2,1)}, u32[]{:S(2)}) %copy-start) | copy-done | bytes 1835032
  16.2 0.0 copy-start.1
  16.2 0.7 copy-done.1
  16.9 1.0 %shard_map.95 = (bf16[256,3584]{1,0:T(8,128)(2,1)S(1)}, f32[4,256]{1,0:T(4,128)S(1)}) custom-call(bf16[256,3584]{1,0:T(8,128)(2,1)S(1)} %bitcast.6, f32[1,3584]{1,0:T(1,128)S(1)} %broadcast_in_dim.3.gain, bf16[4,3584]{1,0:T(4,128)(2,1)S(1)} %bitcast.8), custom_call_target="tpu_custom_call" | custom-call | tf_op jit(solution)/shard_map/pallas_call | solution.py:243
  17.9 0.1 pad_add_fusion.place
  18.0 4.0 %all-to-all-done.received = bf16[16,40,128]{2,1,0:T(8,128)(2,1)S(1)} async-done(((bf16[16,40,128]{2,1,0:T(8,128)(2,1)}), bf16[16,40,128]{2,1,0:T(8,128)(2,1)S(1)}, u32[]{:S(2)}, u32[]{:S(2)}) %all-to-all-start) | async-done | bytes 163872 | tf_op jit(solution)/shard_map/all_to_all | solution.py:254
  22.0 0.0 copy-done.2
  22.0 0.0 copy-done.3
  22.0 1.3 %shard_map.97 = bf16[32,40,128]{2,1,0:T(8,128)(2,1)S(1)} custom-call(s32[3]{0:T(128)S(1)} %pad_add_fusion.place, bf16[256,3584]{1,0:T(8,128)(2,1)S(1)} %get-tuple-element.8.normed, f32[4,256]{1,0:T(4,128)S(1)} %get-tuple-element.9.low, bf16[16,40,128]{2,1,0:T(8,128)(2,1)S(1)} %all-to-all-done.received, f32[8,4]{1,0:T(8,128)S(1)} %copy-done.3, ...), custom_call_target="tpu_custom_call" | custom-call | tf_op jit(solution)/shard_map/pallas_call | solution.py:243
  23.3 23.1 %all_to_all.20.received = bf16[32,40,128]{2,1,0:T(8,128)(2,1)S(1)} all-to-all(bf16[32,40,128]{2,1,0:T(8,128)(2,1)S(1)} %shard_map.97), channel_id=1, replica_groups=mesh['x'=4,'y'=8,'z'=8,'core'=2] {'y','x'}, dimensions={0} | all-to-all | bytes 655360 | tf_op jit(solution)/shard_map/all_to_all | solution.py:254
  46.4 14.6 %all_to_all.21.own = bf16[8,136,128]{2,1,0:T(8,128)(2,1)S(1)} all-to-all(bf16[8,136,128]{2,1,0:T(8,128)(2,1)S(1)} %shard_map.98), channel_id=1, replica_groups=mesh['x'=4,'y'=8,'z'=8,'core'=2] {'z'}, dimensions={0} | all-to-all | bytes 557056 | tf_op jit(solution)/shard_map/all_to_all | solution.py:254
  61.0 1.9 %collective-permute-start = (bf16[8,136,128]{2,1,0:T(8,128)(2,1)S(1)}, bf16[8,136,128]{2,1,0:T(8,128)(2,1)S(1)}, u32[]{:S(2)}, u32[]{:S(2)}) collective-permute-start(bf16[8,136,128]{2,1,0:T(8,128)(2,1)S(1)} %all_to_all.21.own), channel_id=1, source_target_pairs={{0,1},{1,0},{2,3},{3,2},{4,5},{5,4},{6,7},{7,6},{8,9},{9,8},{10,11... | collective-permute-start | bytes 835592 | tf_op jit(solution)/shard_map/ppermute | solution.py:312
  62.9 0.2 shard_map.99.down
  63.1 1.4 %collective-permute-done.other = bf16[8,136,128]{2,1,0:T(8,128)(2,1)S(1)} collective-permute-done((bf16[8,136,128]{2,1,0:T(8,128)(2,1)S(1)}, bf16[8,136,128]{2,1,0:T(8,128)(2,1)S(1)}, u32[]{:S(2)}, u32[]{:S(2)}) %collective-permute-start) | collective-permute-done | bytes 278560 | tf_op jit(solution)/shard_map/ppermute | solution.py:312
  64.4 1.6 %shard_map.100 = (f32[1,1]{1,0:T(1,128)}, bf16[32,56,128]{2,1,0:T(8,128)(2,1)S(1)}) custom-call(s32[3]{0:T(128)S(1)} %pad_add_fusion.place, bf16[8,136,128]{2,1,0:T(8,128)(2,1)S(1)} %all_to_all.21.own, bf16[8,136,128]{2,1,0:T(8,128)(2,1)S(1)} %collective-permute-done.other, bf16[2,128,512]{2,1,0:T(8,128)(2,1)S(1)} %shard_map.99.down), custom_call_target="tpu_custom_call" | custom-call | tf_op jit(solution)/shard_map/pallas_call | solution.py:243
  66.1 21.6 %all_to_all.22.blocks = bf16[32,56,128]{2,1,0:T(8,128)(2,1)S(1)} all-to-all(bf16[32,56,128]{2,1,0:T(8,128)(2,1)S(1)} %get-tuple-element.13), channel_id=1, replica_groups=mesh['x'=4,'y'=8,'z'=8,'core'=2] {'y','x'}, dimensions={0} | all-to-all | bytes 917504 | tf_op jit(solution)/shard_map/all_to_all | solution.py:254
  87.6 1.0 %shard_map.101 = f32[224,1024]{1,0:T(8,128)} custom-call(bf16[32,56,128]{2,1,0:T(8,128)(2,1)S(1)} %all_to_all.22.blocks), custom_call_target="tpu_custom_call" | custom-call | tf_op jit(solution)/shard_map/pallas_call | solution.py:243
  (1 shorter events, 0.0 us)
Async XLA Ops:
  0.6 21.4 %copy-start.2 = (bf16[1,4,1024]{2,1,0:T(4,128)(2,1)S(1)}, bf16[1,4,1024]{2,1,0:T(4,128)(2,1)}, u32[]{:S(2)}) copy-start(bf16[1,4,1024]{2,1,0:T(4,128)(2,1)} %param.14) | copy-start | bytes 24580
  2.8 19.2 %copy-start.3 = (f32[8,4]{1,0:T(8,128)S(1)}, f32[8,4]{1,0:T(8,128)}, u32[]{:S(2)}) copy-start(f32[8,4]{1,0:T(8,128)} %get-tuple-element.11.up_probe) | copy-start | bytes 388
  2.8 19.2 %all-to-all-start = ((bf16[16,40,128]{2,1,0:T(8,128)(2,1)}), bf16[16,40,128]{2,1,0:T(8,128)(2,1)S(1)}, u32[]{:S(2)}, u32[]{:S(2)}) async-start(bf16[16,40,128]{2,1,0:T(8,128)(2,1)} %get-tuple-element.10), calls=%async_computation | async-start | bytes 327680 | tf_op jit(solution)/shard_map/all_to_all | solution.py:254
  14.7 1.5 %copy-start = (bf16[1,256,3584]{2,1,0:T(8,128)(2,1)S(1)}, bf16[1,256,3584]{2,1,0:T(8,128)(2,1)}, u32[]{:S(2)}) copy-start(bf16[1,256,3584]{2,1,0:T(8,128)(2,1)} %param.8) | copy-start | bytes 5505028
  16.2 0.7 copy-start.1
  61.0 3.4 %collective-permute-start = (bf16[8,136,128]{2,1,0:T(8,128)(2,1)S(1)}, bf16[8,136,128]{2,1,0:T(8,128)(2,1)S(1)}, u32[]{:S(2)}, u32[]{:S(2)}) collective-permute-start(bf16[8,136,128]{2,1,0:T(8,128)(2,1)S(1)} %all_to_all.21.own), channel_id=1, source_target_pairs={{0,1},{1,0},{2,3},{3,2},{4,5},{5,4},{6,7},{7,6},{8,9},{9,8},{10,11... | collective-permute-start | bytes 835592 | tf_op jit(solution)/shard_map/ppermute | solution.py:312

commit v5 on v4

--- a/solution.py
+++ b/solution.py
@@ -184,10 +184,11 @@
         jnp.sum(jnp.where(group == float(i), reward, 0.0), axis=0, keepdims=True)
         for i in range(total // GROUP_MEMBERS)
     ]
-    sums = jnp.sum(jnp.concatenate(sums, axis=0), axis=1, keepdims=True) * (1.0 / GROUP_MEMBERS)
-    baseline = jnp.zeros_like(reward)
-    for i in range(total // GROUP_MEMBERS):
-        baseline = jnp.where(group == float(i), sums[i : i + 1, :], baseline)
+    sums = jnp.sum(jnp.transpose(jnp.concatenate(sums, axis=0)), axis=0, keepdims=True) * (1.0 / GROUP_MEMBERS)
+    spare = jnp.zeros((1, LANES - sums.shape[1]), F32)
+    means = jnp.broadcast_to(jnp.concatenate([sums, spare], axis=1), table.shape)
+    chosen = jnp.where(valid, group, 0.0).astype(jnp.int32)
+    baseline = jnp.take_along_axis(means, chosen, axis=1, mode="promise_in_bounds")
     centered = jnp.where(valid, reward - baseline, 0.0)
     spread = sum_all(centered * centered) * (1.0 / total)
     shaped = centered / jnp.sqrt(spread + 1e-05)

time: 89.1 us -> 89.2 us (level)
  no operation moved by 1% of the time
where the time goes in v5:
time: 89.2 us; the launch traced here: 88.7 us
  blocking collectives  59.3 us (66%)
  starting transfers between devices  12.3 us (14%)
  Pallas kernels  7.34 us (8%)
  waiting for transfers between devices  5.33 us (6%)
  local copies, waits for them, and re-layouts  2.98 us (3%)
  between operations  1.37 us (2%)
    all_to_all x3, blocking collectives, exchange(): return lax.all_to_all(array, axes, split_axis=0, concat_axis=0, tiled=True)  59.3 us
    all_to_all x1, starting transfers between devices, exchange(): return lax.all_to_all(array, axes, split_axis=0, concat_axis=0, tiled=True)  10.4 us
    pallas_call x7, Pallas kernels, call(): pl.pallas_call(kernel, out_shape=out_shape, in_specs=in_specs, out_specs=...  7.34 us
    all_to_all x1, waiting for transfers between devices, exchange(): return lax.all_to_all(array, axes, split_axis=0, concat_axis=0, tiled=True)  3.96 us
    unnamed x8, local copies, waits for them, and re-layouts  2.25 us
    ppermute x1, starting transfers between devices, local(): other_ups = lax.ppermute(ups, 'core', [(0, 1), (1, 0)])  1.91 us
  transfers between devices with their start and end apart: 2, of which 2 were waited for; matrix products, arithmetic and copies ran while one was open for 1% of the time, Pallas kernels for 1%

profile of v5, /device:TPU:8, one launch (start us, length us, event | category | flops | bytes accessed | tf_op | source)
XLA Modules:
  0.0 88.7 jit_solution(1602318026622618981)
XLA Ops:
  0.6 0.0 copy-start.2
  0.6 2.2 %shard_map.96 = (f32[8,4]{1,0:T(8,128)}, bf16[16,40,128]{2,1,0:T(8,128)(2,1)}) custom-call(bf16[224,1024]{1,0:T(8,128)(2,1)} %weight_hbm.1, f32[4,128]{1,0:T(4,128)} %keys_hbm.1, f32[4,128]{1,0:T(4,128)} %values_hbm.1, bf16[4,1024]{1,0:T(4,128)(2,1)} %bitcast.9, bf16[4,3584]{1,0:T(4,128)(2,1)} %bitcast.7), custom_call_target="tpu_custom_call" | custom-call | tf_op jit(solution)/shard_map/pallas_call | solution.py:244
  2.8 0.0 copy-start.3
  2.8 10.4 %all-to-all-start = ((bf16[16,40,128]{2,1,0:T(8,128)(2,1)}), bf16[16,40,128]{2,1,0:T(8,128)(2,1)S(1)}, u32[]{:S(2)}, u32[]{:S(2)}) async-start(bf16[16,40,128]{2,1,0:T(8,128)(2,1)} %get-tuple-element.10), calls=%async_computation | async-start | bytes 327680 | tf_op jit(solution)/shard_map/all_to_all | solution.py:255
  13.9 0.7 broadcast_in_dim.3.gain
  14.7 0.0 copy-start
  14.7 1.5 %copy-done = bf16[1,256,3584]{2,1,0:T(8,128)(2,1)S(1)} copy-done((bf16[1,256,3584]{2,1,0:T(8,128)(2,1)S(1)}, bf16[1,256,3584]{2,1,0:T(8,128)(2,1)}, u32[]{:S(2)}) %copy-start) | copy-done | bytes 1835032
  16.2 0.0 copy-start.1
  16.2 0.7 copy-done.1
  16.9 1.0 %shard_map.95 = (bf16[256,3584]{1,0:T(8,128)(2,1)S(1)}, f32[4,256]{1,0:T(4,128)S(1)}) custom-call(bf16[256,3584]{1,0:T(8,128)(2,1)S(1)} %bitcast.6, f32[1,3584]{1,0:T(1,128)S(1)} %broadcast_in_dim.3.gain, bf16[4,3584]{1,0:T(4,128)(2,1)S(1)} %bitcast.8), custom_call_target="tpu_custom_call" | custom-call | tf_op jit(solution)/shard_map/pallas_call | solution.py:244
  17.9 0.1 pad_add_fusion.place
  18.0 4.0 %all-to-all-done.received = bf16[16,40,128]{2,1,0:T(8,128)(2,1)S(1)} async-done(((bf16[16,40,128]{2,1,0:T(8,128)(2,1)}), bf16[16,40,128]{2,1,0:T(8,128)(2,1)S(1)}, u32[]{:S(2)}, u32[]{:S(2)}) %all-to-all-start) | async-done | bytes 163872 | tf_op jit(solution)/shard_map/all_to_all | solution.py:255
  22.0 0.0 copy-done.2
  22.0 0.0 copy-done.3
  22.0 1.3 %shard_map.97 = bf16[32,40,128]{2,1,0:T(8,128)(2,1)S(1)} custom-call(s32[3]{0:T(128)S(1)} %pad_add_fusion.place, bf16[256,3584]{1,0:T(8,128)(2,1)S(1)} %get-tuple-element.8.normed, f32[4,256]{1,0:T(4,128)S(1)} %get-tuple-element.9.low, bf16[16,40,128]{2,1,0:T(8,128)(2,1)S(1)} %all-to-all-done.received, f32[8,4]{1,0:T(8,128)S(1)} %copy-done.3, ...), custom_call_target="tpu_custom_call" | custom-call | tf_op jit(solution)/shard_map/pallas_call | solution.py:244
  23.3 23.1 %all_to_all.20.received = bf16[32,40,128]{2,1,0:T(8,128)(2,1)S(1)} all-to-all(bf16[32,40,128]{2,1,0:T(8,128)(2,1)S(1)} %shard_map.97), channel_id=1, replica_groups=mesh['x'=4,'y'=8,'z'=8,'core'=2] {'y','x'}, dimensions={0} | all-to-all | bytes 655360 | tf_op jit(solution)/shard_map/all_to_all | solution.py:255
  46.4 14.6 %all_to_all.21.own = bf16[8,136,128]{2,1,0:T(8,128)(2,1)S(1)} all-to-all(bf16[8,136,128]{2,1,0:T(8,128)(2,1)S(1)} %shard_map.98), channel_id=1, replica_groups=mesh['x'=4,'y'=8,'z'=8,'core'=2] {'z'}, dimensions={0} | all-to-all | bytes 557056 | tf_op jit(solution)/shard_map/all_to_all | solution.py:255
  61.0 1.9 %collective-permute-start = (bf16[8,136,128]{2,1,0:T(8,128)(2,1)S(1)}, bf16[8,136,128]{2,1,0:T(8,128)(2,1)S(1)}, u32[]{:S(2)}, u32[]{:S(2)}) collective-permute-start(bf16[8,136,128]{2,1,0:T(8,128)(2,1)S(1)} %all_to_all.21.own), channel_id=1, source_target_pairs={{0,1},{1,0},{2,3},{3,2},{4,5},{5,4},{6,7},{7,6},{8,9},{9,8},{10,11... | collective-permute-start | bytes 835592 | tf_op jit(solution)/shard_map/ppermute | solution.py:313
  62.9 0.2 shard_map.99.down
  63.1 1.4 %collective-permute-done.other = bf16[8,136,128]{2,1,0:T(8,128)(2,1)S(1)} collective-permute-done((bf16[8,136,128]{2,1,0:T(8,128)(2,1)S(1)}, bf16[8,136,128]{2,1,0:T(8,128)(2,1)S(1)}, u32[]{:S(2)}, u32[]{:S(2)}) %collective-permute-start) | collective-permute-done | bytes 278560 | tf_op jit(solution)/shard_map/ppermute | solution.py:313
  64.4 1.7 %shard_map.100 = (f32[1,1]{1,0:T(1,128)}, bf16[32,56,128]{2,1,0:T(8,128)(2,1)S(1)}) custom-call(s32[3]{0:T(128)S(1)} %pad_add_fusion.place, bf16[8,136,128]{2,1,0:T(8,128)(2,1)S(1)} %all_to_all.21.own, bf16[8,136,128]{2,1,0:T(8,128)(2,1)S(1)} %collective-permute-done.other, bf16[2,128,512]{2,1,0:T(8,128)(2,1)S(1)} %shard_map.99.down), custom_call_target="tpu_custom_call" | custom-call | tf_op jit(solution)/shard_map/pallas_call | solution.py:244
  66.2 21.6 %all_to_all.22.blocks = bf16[32,56,128]{2,1,0:T(8,128)(2,1)S(1)} all-to-all(bf16[32,56,128]{2,1,0:T(8,128)(2,1)S(1)} %get-tuple-element.13), channel_id=1, replica_groups=mesh['x'=4,'y'=8,'z'=8,'core'=2] {'y','x'}, dimensions={0} | all-to-all | bytes 917504 | tf_op jit(solution)/shard_map/all_to_all | solution.py:255
  87.7 1.0 %shard_map.101 = f32[224,1024]{1,0:T(8,128)} custom-call(bf16[32,56,128]{2,1,0:T(8,128)(2,1)S(1)} %all_to_all.22.blocks), custom_call_target="tpu_custom_call" | custom-call | tf_op jit(solution)/shard_map/pallas_call | solution.py:244
  (1 shorter events, 0.0 us)
Async XLA Ops:
  0.6 21.4 %copy-start.2 = (bf16[1,4,1024]{2,1,0:T(4,128)(2,1)S(1)}, bf16[1,4,1024]{2,1,0:T(4,128)(2,1)}, u32[]{:S(2)}) copy-start(bf16[1,4,1024]{2,1,0:T(4,128)(2,1)} %param.14) | copy-start | bytes 24580
  2.8 19.2 %copy-start.3 = (f32[8,4]{1,0:T(8,128)S(1)}, f32[8,4]{1,0:T(8,128)}, u32[]{:S(2)}) copy-start(f32[8,4]{1,0:T(8,128)} %get-tuple-element.11.up_probe) | copy-start | bytes 388
  2.8 19.2 %all-to-all-start = ((bf16[16,40,128]{2,1,0:T(8,128)(2,1)}), bf16[16,40,128]{2,1,0:T(8,128)(2,1)S(1)}, u32[]{:S(2)}, u32[]{:S(2)}) async-start(bf16[16,40,128]{2,1,0:T(8,128)(2,1)} %get-tuple-element.10), calls=%async_computation | async-start | bytes 327680 | tf_op jit(solution)/shard_map/all_to_all | solution.py:255
  14.7 1.5 %copy-start = (bf16[1,256,3584]{2,1,0:T(8,128)(2,1)S(1)}, bf16[1,256,3584]{2,1,0:T(8,128)(2,1)}, u32[]{:S(2)}) copy-start(bf16[1,256,3584]{2,1,0:T(8,128)(2,1)} %param.8) | copy-start | bytes 5505028
  16.2 0.7 copy-start.1
  61.0 3.4 %collective-permute-start = (bf16[8,136,128]{2,1,0:T(8,128)(2,1)S(1)}, bf16[8,136,128]{2,1,0:T(8,128)(2,1)S(1)}, u32[]{:S(2)}, u32[]{:S(2)}) collective-permute-start(bf16[8,136,128]{2,1,0:T(8,128)(2,1)S(1)} %all_to_all.21.own), channel_id=1, source_target_pairs={{0,1},{1,0},{2,3},{3,2},{4,5},{5,4},{6,7},{7,6},{8,9},{9,8},{10,11... | collective-permute-start | bytes 835592 | tf_op jit(solution)/shard_map/ppermute | solution.py:313
